TPU v7x, 128 devices: a whole 4x4x4 slice. The times are simulated.
128 devices in a mesh: fsdp: 4 (over x), ctx: 4 (over y_lo, core), tp: 8 (over y_hi, z).
Axes of the slice: x: 4, y: 4 (y_hi: 2, y_lo: 2; y = y_hi * 2 + y_lo), z: 4, core: 2. Of those that a mesh axis runs over, the one named last changes fastest.
Arguments:
- tokens: bfloat16 [8, 1024, 2048], P('fsdp', 'ctx'), may hold values from -6 to 6
- block_order: int32 [8], replicated, may hold values from 0 to 7, each once
- cotangent: bfloat16 [8, 1024, 2048], P('fsdp', 'ctx'), may hold values from -6 to 6
- qkv_weight: bfloat16 [2, 2048, 6144], P(None, ('fsdp', 'ctx'), 'tp'), may hold values from -0.125 to 0.125
- qkv_bias: bfloat16 [2, 6144], P(None, 'tp'), may hold values from -1.1953125 to 1.1953125
- dense_weight: bfloat16 [2, 2048, 2048], P(None, ('fsdp', 'ctx'), 'tp'), may hold values from -0.75 to 0.75
- up_weight: bfloat16 [2, 2048, 8192], P(None, ('fsdp', 'ctx'), 'tp'), may hold values from -0.125 to 0.125
- up_bias: bfloat16 [2, 8192], P(None, 'tp'), may hold values from -1.1953125 to 1.1953125
- down_weight: bfloat16 [2, 2048, 8192], P(None, ('fsdp', 'ctx'), 'tp'), may hold values from -0.0625 to 0.0625
- norm_gains: bfloat16 [2, 2, 2048], replicated, may hold values from 0.5 to 1.5
- norm_shifts: bfloat16 [2, 2, 2048], replicated, may hold values from -1.1953125 to 1.1953125
- out_bias: bfloat16 [2, 2048], replicated, may hold values from -1.1953125 to 1.1953125
Outputs:
- activations: float32 [8, 1024, 2048], P('fsdp', 'ctx')
- input_grad: float32 [8, 1024, 2048], P('fsdp', 'ctx')
- qkv_weight_grad: float32 [2, 2048, 6144], P(None, ('fsdp', 'ctx'), 'tp')
- qkv_bias_grad: float32 [2, 6144], P(None, 'tp')
- dense_weight_grad: float32 [2, 2048, 2048], P(None, ('fsdp', 'ctx'), 'tp')
- up_weight_grad: float32 [2, 2048, 8192], P(None, ('fsdp', 'ctx'), 'tp')
- up_bias_grad: float32 [2, 8192], P(None, 'tp')
- down_weight_grad: float32 [2, 2048, 8192], P(None, ('fsdp', 'ctx'), 'tp')
- norm_gains_grad: float32 [2, 2, 2048], replicated
- norm_shifts_grad: float32 [2, 2, 2048], replicated
- out_bias_grad: float32 [2, 2048], replicated
Inputs may be any that keep to these rules, and one draw needn't show every extreme that they name: Each of 0 to 2 * 4 - 1 appears once; block slot j of a sequence (rows j * 128 to j * 128 + 127) holds positions block_order[j] * 128 onward, for every sequence.
All inputs are finite; a program needn't handle non-finite values.
Results may differ from a plain program's by a relative error of at most 0.023.
Values may be sent and summed in bfloat16 or wider, within the bound.
No kernel may reach another device: no remote copies, remote signals or barrier semaphores. Data moves between devices by JAX's collectives and lax.ppermute only.
A program may use at most 192 MiB of HBM per device.

v0:
```python
import jax
import jax.numpy as jnp
from jax import lax
from jax.experimental import pallas as pl
from jax.experimental.pallas import tpu as pltpu
from jax.sharding import PartitionSpec as P

HD = 256
ROT = 64
LAYERS = 2
EPSILON = 1e-05
LANES = 128
TILE = 256
CHUNK = 32
ALL_PANELS = (0, 3, 4, 8)
IN_PANELS, OUT_PANELS = (0, 3), (0, 1)
F32 = jnp.float32
BF16 = jnp.bfloat16
VMEM_LIMIT = 24 * 1024 * 1024


def swap_core(value):
    return lax.ppermute(value, "ctx", [(i, i ^ 1) for i in range(4)])


def swap_y(value):
    return lax.ppermute(value, "ctx", [(i, i ^ 2) for i in range(4)])


def from_x(value, k):
    return lax.ppermute(value, "fsdp", [((i + k) % 4, i) for i in range(4)])


def swap_both(value):
    return lax.ppermute(value, "ctx", [(i, i ^ 3) for i in range(4)])


def swap_tp(value, k):
    return lax.ppermute(value, "tp", [(i, i ^ k) for i in range(8)])


def from_z(value, k):
    return lax.ppermute(value, "tp", [((i & 4) + (i + k) % 4, i) for i in range(8)])


def to_z(value, k):
    return lax.ppermute(value, "tp", [(i, (i & 4) + (i + k) % 4) for i in range(8)])


def gather_weights(shard):
    return lax.all_gather(shard, ("fsdp", "ctx"), axis=1, tiled=True)


def together(*values):
    return lax.optimization_barrier(values)


def tp_1(pieces):
    firsts = [to_z(pieces[k], k) for k in (1, 3, 2)]
    return (pieces[0], pieces[4]), (firsts, swap_tp(pieces[5], 4))


def tp_2(kept, arrived):
    (own, near), (firsts, far) = kept, arrived
    first = add_up(own, *firsts)
    parts = add_split(near, far)
    seconds = [to_z(parts[k], k) for k in (1, 3, 2)]
    return (first, parts[0]), (swap_tp(first, 4), seconds)


def tp_3_sums(kept, arrived):
    (first, own), (other, seconds) = kept, arrived
    second = add_up(own, *seconds)
    return add_up(first, other), second


def tp_3(kept, arrived):
    first, second = tp_3_sums(kept, arrived)
    seconds = [from_z(second, k) for k in (1, 3, 2)]
    firsts = [from_z(first, k) for k in (1, 3, 2)]
    return (first, second), (firsts, seconds)


def tp_4(second, seconds):
    near = stack_up(second, seconds[0], seconds[2], seconds[1])
    return near, swap_tp(near, 4)


def tp_pieces(first, firsts, near, far):
    return (first, firsts[0], firsts[2], firsts[1], near, far)


def around(value, move):
    return [move(value, k) for k in (1, 2, 3)]


def around_ctx(value):
    return [swap_y(value), swap_core(value), swap_both(value)]


def pair_up(value, got):
    return (value + got[1]) + (got[0] + got[2])


def call(body, grid, ins, in_specs, outs, out_specs, scratch=(), prefetch=0, flops=0):
    nbytes = sum(a.size * a.dtype.itemsize for a in outs)
    nbytes += sum(min(a.size * a.dtype.itemsize, 1 << 22) for a in ins)
    return pl.pallas_call(
        body,
        grid_spec=pltpu.PrefetchScalarGridSpec(
            num_scalar_prefetch=prefetch,
            grid=grid,
            in_specs=in_specs,
            out_specs=out_specs,
            scratch_shapes=scratch,
        ),
        out_shape=outs,
        compiler_params=pltpu.CompilerParams(vmem_limit_bytes=VMEM_LIMIT),
        cost_estimate=pl.CostEstimate(
            flops=int(flops), bytes_accessed=int(nbytes), transcendentals=0
        ),
    )(*ins)


def call_once(body, ins, outs, scratch=(), prefetch=0, hbm=(), out_hbm=False, flops=0):
    ins = tuple(
        pltpu.with_memory_space_constraint(a, pltpu.HBM) if i in hbm else a
        for i, a in enumerate(ins)
    )
    specs = [
        pl.BlockSpec(memory_space=pltpu.HBM) if i in hbm else whole(a)
        for i, a in enumerate(ins)
        if i >= prefetch
    ]
    out_specs = [pl.BlockSpec(memory_space=pltpu.HBM) if out_hbm else whole(a) for a in outs]
    return call(body, (1,), ins, specs, outs, out_specs, scratch, prefetch, flops)


def pinned(*arrays):
    return tuple(pltpu.with_memory_space_constraint(a, pltpu.HBM) for a in arrays)


def shape(dims, dtype):
    return jax.ShapeDtypeStruct(dims, dtype)


def whole(a):
    return pl.BlockSpec(a.shape, lambda *_: (0,) * len(a.shape))


def dot_nn(a, b):
    return lax.dot_general(a, b, (((1,), (0,)), ((), ())), preferred_element_type=F32)


def dot_nt(a, b):
    return lax.dot_general(a, b, (((1,), (1,)), ((), ())), preferred_element_type=F32)


def dot_tn(a, b):
    return lax.dot_general(a, b, (((0,), (0,)), ((), ())), preferred_element_type=F32)


def fold_rows(a):
    return jnp.sum(a.reshape(a.shape[0] // 8, 8, a.shape[1]), axis=0)


def sum_rows(a):
    return jnp.sum(a, axis=0, keepdims=True)


def span(j, size):
    return pl.ds(pl.multiple_of(j * size, size), size)


def start(copies):
    for copy in copies:
        copy.start()


def wait(copies):
    for copy in copies:
        copy.wait()


def load_panels(w_ref, first, scratch, sems, at=0):
    return [
        pltpu.make_async_copy(w_ref.at[first + i], scratch.at[at + i], sems.at[at + i])
        for i in range(scratch.shape[0] - at)
    ]


def panels_scratch(n, width):
    return [pltpu.VMEM((n, width, TILE), BF16), pltpu.SemaphoreType.DMA((n,))]


class Tiles:
    def __init__(self, w_ref, runs, scratch, sems):
        self.w_ref, self.runs, self.scratch, self.sems = w_ref, runs, scratch, sems

    def copies(self, j):
        at = 0
        for i, (first, n) in enumerate(self.runs):
            yield pltpu.make_async_copy(
                self.w_ref.at[first : first + n, span(j, TILE), :],
                self.scratch.at[j, at : at + n],
                self.sems.at[i, j],
            )
            at += n

    def start(self):
        def step(j, carry):
            start(self.copies(j))
            return carry

        lax.fori_loop(0, self.scratch.shape[0], step, 0)

    def get(self, j):
        wait(self.copies(j))
        n = self.scratch.shape[1]
        return [self.scratch[j, i] for i in range(n)]


def tiles_scratch(runs, width):
    n = sum(size for _, size in runs)
    return [
        pltpu.VMEM((width // TILE, n, TILE, TILE), BF16),
        pltpu.SemaphoreType.DMA((len(runs), width // TILE)),
    ]


def row_copies(source, row_ref, target, sems, back=False):
    per = source.shape[1] // CHUNK

    def copy(k):
        far = source.at[k // per, span(row_ref[k], CHUNK)]
        own = target.at[span(k, CHUNK)]
        ends = (own, far) if back else (far, own)
        return pltpu.make_async_copy(*ends, sems.at[k])

    return copy


def for_chunks(n, step, carry=0):
    return lax.fori_loop(0, n, step, carry)


class Rows:
    def __init__(self, refs, scratch, sems):
        self.scratch, self.sems = scratch, sems
        self.parts, base = [], 0
        for ref in refs:
            self.parts.append((ref, base, ref.shape[0] // CHUNK))
            base += ref.shape[0] // CHUNK

    def copy(self, part, i):
        ref, base, _ = part
        return pltpu.make_async_copy(
            ref.at[span(i, CHUNK)], self.scratch.at[span(base + i, CHUNK)], self.sems.at[base + i]
        )


def start_rows(*rows):
    order = [(base + i, r, (ref, base, n), i) for r in rows for ref, base, n in r.parts for i in range(n)]
    for _, r, part, i in sorted(order, key=lambda entry: entry[0]):
        r.copy(part, i).start()


def for_rows(pieces, others, fn, carry=0):
    for part in pieces.parts:

        def step(i, carry, part=part):
            pieces.copy(part, i).wait()
            for other in others:
                other.copy(other.parts[0], part[1] + i).wait()
            at = span(part[1] + i, CHUNK)
            return fn(part[1] + i, pieces.scratch[at, :].astype(F32), carry)

        carry = lax.fori_loop(0, part[2], step, carry)
    return carry


def rows_scratch(rows, width, n=1):
    one = [pltpu.VMEM((rows, width), BF16), pltpu.SemaphoreType.DMA((rows // CHUNK,))]
    return one * n


def piece_shapes(rows, width):
    return [shape((rows // 8, width), BF16)] * 4 + [shape((rows // 4, width), BF16)] * 2


def put_pieces(at, y, refs):
    base = 0
    for ref in refs:
        ref[:, at] = y[base : base + ref.shape[0]].astype(BF16)
        base += ref.shape[0]


def put_norms(at, x, vec_ref, layer, stat_ref, na_ref, nm_ref):
    mean = jnp.mean(x, axis=1, keepdims=True)
    center = x - mean
    r = lax.rsqrt(jnp.mean(center * center, axis=1, keepdims=True) + EPSILON)
    u = center * r
    lane = lax.broadcasted_iota(jnp.int32, (x.shape[0], LANES), 1)
    stat_ref[at, :] = jnp.where(lane < LANES // 2, mean, r)
    na_ref[at, :] = (u * vec_ref[layer, 0:1] + vec_ref[layer, 2:3]).astype(BF16)
    nm_ref[at, :] = (u * vec_ref[layer, 1:2] + vec_ref[layer, 3:4]).astype(BF16)


def unit_of(x, stats):
    return (x.astype(F32) - stats[:, 0:1]) * stats[:, LANES // 2 : LANES // 2 + 1]


def put_qkv(na_ref, loads, w_ref, b_ref, t_ref, q_ref, kv_ref):
    for j in range(3):
        loads[j].wait()
        y = dot_nn(na_ref[...], w_ref[j]) + b_ref[:, j * HD : (j + 1) * HD]
        if j == 0:
            q_ref[...] = turn(y, t_ref, 1.0).astype(BF16)
        elif j == 1:
            kv_ref[:, :HD] = turn(y, t_ref, 1.0).astype(BF16)
        else:
            kv_ref[:, HD:] = y.astype(BF16)


def in_outs(rows, width):
    return [
        shape((rows, width), BF16),
        shape((rows, LANES), F32),
        shape((rows, width), BF16),
        shape((rows, width), BF16),
        shape((rows, HD), BF16),
        shape((rows, 2 * HD), BF16),
    ]


def first_in(tokens, row_at, vec, w, bias, tables):
    width = tokens.shape[2]
    rows = tokens.shape[0] * tokens.shape[1]

    def body(
        row_ref,
        tok_ref,
        vec_ref,
        w_ref,
        b_ref,
        t_ref,
        x_ref,
        stat_ref,
        na_ref,
        nm_ref,
        q_ref,
        kv_ref,
        panels,
        sems,
        row_sems,
    ):
        news = row_copies(tok_ref, row_ref, x_ref, row_sems)
        for k in range(rows // CHUNK):
            news(k).start()
        loads = load_panels(w_ref, w[1], panels, sems)
        start(loads)

        def step(i, carry):
            news(i).wait()
            at = span(i, CHUNK)
            put_norms(at, x_ref[at, :].astype(F32), vec_ref, 0, stat_ref, na_ref, nm_ref)
            return carry

        for_chunks(rows // CHUNK, step)
        put_qkv(na_ref, loads, panels, b_ref, t_ref, q_ref, kv_ref)

    return call_once(
        body,
        (row_at, tokens, vec, w[0], bias, tables),
        in_outs(rows, width),
        panels_scratch(3, width) + [pltpu.SemaphoreType.DMA((rows // CHUNK,))],
        prefetch=1,
        hbm=(1, 3),
        flops=2 * rows * width * 3 * HD,
    )


def next_in(x, pieces, layer, vec, w, bias, tables):
    rows, width = x.shape

    def body(x_ref, *rest):
        refs = rest[:6]
        vec_ref, w_ref, b_ref, t_ref, new_ref, stat_ref, na_ref, nm_ref = rest[6:14]
        q_ref, kv_ref, panels, sems, xs, x_sems, ps, p_sems = rest[14:]
        xs, ps = Rows([x_ref], xs, x_sems), Rows(refs, ps, p_sems)
        start_rows(xs, ps)
        loads = load_panels(w_ref, w[1], panels, sems)
        start(loads)

        def step(i, branch, carry):
            at = span(i, CHUNK)
            new = xs.scratch[at, :].astype(F32) + branch + vec_ref[layer - 1, 4:5]
            new_ref[at, :] = new.astype(BF16)
            put_norms(at, new, vec_ref, layer, stat_ref, na_ref, nm_ref)
            return carry

        for_rows(ps, [xs], step)
        put_qkv(na_ref, loads, panels, b_ref, t_ref, q_ref, kv_ref)

    return call_once(
        body,
        (x, *pieces, vec, w[0], bias, tables),
        in_outs(rows, width),
        panels_scratch(3, width) + rows_scratch(rows, width, 2),
        hbm=(0, 1, 2, 3, 4, 5, 6, 8),
        flops=2 * rows * width * 3 * HD,
    )


def gelu_parts(h):
    e = jnp.exp(-0.5 * h * h)
    t = 1.0 / (1.0 + (0.3275911 * 0.5**0.5) * jnp.abs(h))
    tail = 1.061405429 * t - 1.453152027
    tail = tail * t + 1.421413741
    tail = tail * t - 0.284496736
    tail = (tail * t + 0.254829592) * t * (0.5 * e)
    return jnp.where(h >= 0, 1.0 - tail, tail), e * 0.3989422804014327


def project_up(nm, w, bias):
    rows, width = nm.shape
    hidden = bias.shape[1]

    def body(n_ref, w_ref, b_ref, act_ref, slope_ref, panels, sems):
        loads = load_panels(w_ref, w[2], panels, sems)
        start(loads)
        for j in range(hidden // TILE):
            at = slice(j * TILE, (j + 1) * TILE)
            loads[j].wait()
            h = dot_nn(n_ref[...], panels[j]) + b_ref[:, at]
            cdf, density = gelu_parts(h)
            act_ref[:, at] = (h * cdf).astype(BF16)
            slope_ref[:, at] = (cdf + h * density).astype(BF16)

    return call_once(
        body,
        (nm, w[0], bias),
        [shape((rows, hidden), BF16), shape((rows, hidden), BF16)],
        panels_scratch(hidden // TILE, width),
        hbm=(1,),
        flops=2 * rows * width * hidden,
    )


def weights_of(q, kvs, qpos, kpos):
    scores = [dot_nt(q, kv[:, :HD]) * HD**-0.5 for kv in kvs]
    scores = jnp.concatenate(scores, axis=1)
    scores = jnp.where(kpos <= qpos, scores, -1e30)
    e = jnp.exp(scores - jnp.max(scores, axis=1, keepdims=True))
    return e / jnp.sum(e, axis=1, keepdims=True)


def attend_out(q, kvs, qpos, kpos, active, w):
    rows, hidden = active.shape
    width = w[0].shape[1]
    seqs = kpos.shape[0]
    per = rows // seqs
    runs = [(w[1], 1), (w[2], hidden // TILE)]

    def body(q_ref, k0, k1, k2, k3, qp_ref, kp_ref, act_ref, w_ref, mixed_ref, *rest):
        refs = rest[:6]
        wide, sems, left = rest[6:]
        tiles = Tiles(w_ref, runs, wide, sems)
        tiles.start()
        for s in range(seqs):
            at = slice(s * per, (s + 1) * per)
            kvs = [ref[at] for ref in (k0, k1, k2, k3)]
            p = weights_of(q_ref[at], kvs, qp_ref[at], kp_ref[s : s + 1]).astype(BF16)
            mixed = sum(dot_nn(p[:, i * per : (i + 1) * per], kvs[i][:, HD:]) for i in range(4))
            mixed_ref[at] = mixed.astype(BF16)
        left[:, :HD] = mixed_ref[...]
        left[:, HD:] = act_ref[...]

        def step(j, carry):
            y = dot_nt(left[...], jnp.concatenate(tiles.get(j), axis=1))
            put_pieces(span(j, TILE), y, refs)
            return carry

        lax.fori_loop(0, width // TILE, step, 0)

    out = call_once(
        body,
        (q, *kvs, qpos, kpos, active, w[0]),
        [shape((rows, HD), BF16)] + piece_shapes(rows, width),
        tiles_scratch(runs, width) + [pltpu.VMEM((rows, HD + hidden), BF16)],
        hbm=(8,),
        flops=16 * rows * per * HD + 2 * rows * width * (HD + hidden),
    )
    return out[0], out[1:]


def put_back_out(gb_ref, loads, panels, slope_ref, gm_ref, gh_ref, part_ref):
    for j in range(panels.shape[0]):
        loads[j].wait()
        y = dot_nn(gb_ref[...], panels[j])
        if j == 0:
            gm_ref[...] = y.astype(BF16)
        else:
            at = slice((j - 1) * TILE, j * TILE)
            gh = (y * slope_ref[:, at].astype(F32)).astype(BF16)
            gh_ref[:, at] = gh
            part_ref[6:7, at] = sum_rows(gh.astype(F32))


def load_back_out(w_ref, w, panels, sems):
    first = pltpu.make_async_copy(w_ref.at[w[1]], panels.at[0], sems.at[0])
    return [first] + load_panels(w_ref, w[2], panels, sems, at=1)


def back_out_shapes(rows, width, hidden):
    return [
        shape((rows, width), BF16),
        shape((rows, HD), BF16),
        shape((rows, hidden), BF16),
        shape((8, width), F32),
    ]


def last_back_out(cotangent, row_at, w, slope):
    width = cotangent.shape[2]
    rows, hidden = slope.shape
    n = 1 + hidden // TILE

    def body(
        row_ref, cot_ref, w_ref, slope_ref, gb_ref, gm_ref, gh_ref, part_ref, panels, sems, row_sems
    ):
        news = row_copies(cot_ref, row_ref, gb_ref, row_sems)
        for k in range(rows // CHUNK):
            news(k).start()
        loads = load_back_out(w_ref, w, panels, sems)
        start(loads)
        part_ref[...] = jnp.zeros_like(part_ref)

        def step(i, total):
            news(i).wait()
            return total + fold_rows(gb_ref[span(i, CHUNK), :].astype(F32))

        total = for_chunks(rows // CHUNK, step, jnp.zeros((8, width), F32))
        part_ref[4:5, :] = sum_rows(total)
        put_back_out(gb_ref, loads, panels, slope_ref, gm_ref, gh_ref, part_ref)

    return call_once(
        body,
        (row_at, cotangent, w[0], *pinned(slope)),
        back_out_shapes(rows, width, hidden),
        panels_scratch(n, width) + [pltpu.SemaphoreType.DMA((rows // CHUNK,))],
        prefetch=1,
        hbm=(1, 2),
        flops=2 * rows * width * n * TILE,
    )


def grad_in(g, x, stats, total):
    u = unit_of(x, stats)
    back = total - jnp.mean(total, axis=1, keepdims=True)
    back = back - u * jnp.mean(total * u, axis=1, keepdims=True)
    return g.astype(F32) + stats[:, LANES // 2 : LANES // 2 + 1] * back


def next_back_out(g, x, stats, pieces, w, slope):
    rows, width = g.shape
    hidden = slope.shape[1]
    n = 1 + hidden // TILE

    def body(g_ref, x_ref, stat_ref, *rest):
        refs = rest[:6]
        w_ref, slope_ref, gb_ref, gm_ref, gh_ref, part_ref, panels, sems = rest[6:14]
        gs, xs, ps = (
            Rows(r, rest[14 + 2 * i], rest[15 + 2 * i])
            for i, r in enumerate(([g_ref], [x_ref], refs))
        )
        start_rows(gs, xs, ps)
        loads = load_back_out(w_ref, w, panels, sems)
        start(loads)
        part_ref[...] = jnp.zeros_like(part_ref)

        def step(i, branch, total):
            at = span(i, CHUNK)
            new = grad_in(gs.scratch[at, :], xs.scratch[at, :], stat_ref[at, :], branch)
            gb_ref[at, :] = new.astype(BF16)
            return total + fold_rows(new)

        total = for_rows(ps, [gs, xs], step, jnp.zeros((8, width), F32))
        part_ref[4:5, :] = sum_rows(total)
        put_back_out(gb_ref, loads, panels, slope_ref, gm_ref, gh_ref, part_ref)

    return call_once(
        body,
        (g, x, stats, *pieces, w[0], *pinned(slope)),
        back_out_shapes(rows, width, hidden),
        panels_scratch(n, width) + rows_scratch(rows, width, 3),
        hbm=(0, 1, 3, 4, 5, 6, 7, 8, 9),
        flops=2 * rows * width * n * TILE,
    )


def attend_back(q, kvs, gm, qpos, kpos):
    rows = q.shape[0]
    seqs = kpos.shape[0]
    per = rows // seqs

    def body(q_ref, k0, k1, k2, k3, gm_ref, qp_ref, kp_ref, dq_ref, own_ref, y_ref, send_ref):
        part = [slice(i * per, (i + 1) * per) for i in range(4)]
        for s in range(seqs):
            at = part[s]
            kvs = [ref[at] for ref in (k0, k1, k2, k3)]
            q = q_ref[at]
            gm = gm_ref[at]
            p = weights_of(q, kvs, qp_ref[at], kp_ref[s : s + 1])
            dp = jnp.concatenate([dot_nt(gm, kv[:, HD:]) for kv in kvs], axis=1)
            ds = (p * (dp - jnp.sum(p * dp, axis=1, keepdims=True))).astype(BF16)
            p = p.astype(BF16)
            dq = sum(dot_nn(ds[:, part[i]], kvs[i][:, :HD]) for i in range(4))
            dq_ref[at] = dq * HD**-0.5
            late = slice(rows + s * per, rows + (s + 1) * per)
            places = (own_ref.at[at], send_ref.at[at], y_ref.at[at], send_ref.at[late])
            for i, ref in enumerate(places):
                ref[:, :HD] = (dot_tn(ds[:, part[i]], q) * HD**-0.5).astype(ref.dtype)
                ref[:, HD:] = dot_tn(p[:, part[i]], gm).astype(ref.dtype)

    return call_once(
        body,
        (q, *pinned(*kvs), gm, qpos, kpos),
        [
            shape((rows, HD), F32),
            shape((rows, 2 * HD), F32),
            shape((rows, 2 * HD), F32),
            shape((2 * rows, 2 * HD), BF16),
        ],
        flops=40 * rows * per * HD,
    )


def back_in(dq, own, from_core, from_y, tables, gh, w, x, stats, vec, layer, part):
    rows, hidden = gh.shape
    width = w[0].shape[1]
    runs = [(w[1], 3), (w[2], hidden // TILE)]

    def body(
        dq_ref,
        own_ref,
        core_ref,
        y_ref,
        t_ref,
        gh_ref,
        w_ref,
        x_ref,
        stat_ref,
        vec_ref,
        part_ref,
        gp_ref,
        *rest,
    ):
        refs = rest[:6]
        sum_ref, wide, sems, xs, x_sems = rest[6:]
        tiles = Tiles(w_ref, runs, wide, sems)

        def x_copy(j):
            at = span(j, TILE)
            return pltpu.make_async_copy(x_ref.at[:, at], xs.at[j], x_sems.at[j])

        def begin(j, carry):
            start(tiles.copies(j))
            x_copy(j).start()
            return carry

        lax.fori_loop(0, width // TILE, begin, 0)
        both = own_ref[...] + core_ref[:rows].astype(F32) + y_ref[...].astype(F32)
        parts = (turn(dq_ref[...], t_ref, -1.0), turn(both[:, :HD], t_ref, -1.0), both[:, HD:])
        sum_ref[...] = part_ref[...]
        for i, a in enumerate(parts):
            a = a.astype(BF16)
            at = slice(i * HD, (i + 1) * HD)
            gp_ref[:, at] = a
            sum_ref[5:6, at] = sum_rows(a.astype(F32))

        def step(j, carry):
            at = span(j, TILE)
            w_tile = tiles.get(j)
            gna = dot_nt(gp_ref[...], jnp.concatenate(w_tile[:3], axis=1))
            gnm = dot_nt(gh_ref[...], jnp.concatenate(w_tile[3:], axis=1))
            x_copy(j).wait()
            u = unit_of(xs[j], stat_ref[...])
            y = gna * vec_ref[layer, 0:1, at] + gnm * vec_ref[layer, 1:2, at]
            put_pieces(at, y, refs)
            for i, a in enumerate((gna * u, gnm * u, gna, gnm)):
                sum_ref[i : i + 1, at] = sum_rows(a)
            return carry

        lax.fori_loop(0, width // TILE, step, 0)

    out = call_once(
        body,
        (*pinned(dq, own, from_core), from_y, tables, *pinned(gh), w[0], x, stats, vec, part),
        [shape((rows, 3 * HD), BF16)] + piece_shapes(rows, width) + [shape((8, width), F32)],
        tiles_scratch(runs, width)
        + [pltpu.VMEM((width // TILE, rows, TILE), BF16), pltpu.SemaphoreType.DMA((width // TILE,))],
        hbm=(6, 7),
        flops=2 * rows * width * (3 * HD + hidden),
    )
    return out[0], out[1:7], out[7]


def put_rows(like, row_at, rows_in, pieces, others, value):
    seqs, per, width = like.shape
    rows = seqs * per
    n = len(rows_in)

    def body(row_ref, *rest):
        refs = rest[: n + 6 + len(others)]
        out_ref, own, sems = rest[len(refs) : len(refs) + 3]
        rest = rest[len(refs) + 3 :]
        loads = [Rows([refs[i]], rest[2 * i], rest[2 * i + 1]) for i in range(n)]
        ps = Rows(refs[n : n + 6], rest[2 * n], rest[2 * n + 1])
        start_rows(*loads, ps)
        copies = row_copies(out_ref, row_ref, own, sems, back=True)

        def step(i, branch, carry):
            at = span(i, CHUNK)
            chunks = [load.scratch[at, :] for load in loads]
            own[at, :] = value(chunks, branch, at, refs[n + 6 :])
            copies(i).start()
            return carry

        for_rows(ps, loads, step)

        def finish(i, carry):
            copies(i).wait()
            return carry

        for_chunks(rows // CHUNK, finish)

    return call_once(
        body,
        (row_at, *rows_in, *pieces, *others),
        [shape((seqs, per, width), F32)],
        [pltpu.VMEM((rows, width), F32), pltpu.SemaphoreType.DMA((rows // CHUNK,))]
        + rows_scratch(rows, width, n + 1),
        prefetch=1,
        hbm=tuple(range(1, n + 7)),
        out_hbm=True,
    )[0]


def last_stream(like, row_at, x, pieces, vec, layer):
    def value(chunks, branch, at, others):
        return chunks[0].astype(F32) + branch + others[0][layer, 4:5]

    return put_rows(like, row_at, (x,), pieces, (vec,), value)


def last_grad(like, row_at, g, x, stats, pieces):
    def value(chunks, branch, at, others):
        return grad_in(chunks[0], chunks[1], others[0][at, :], branch)

    return put_rows(like, row_at, (g, x), pieces, (stats,), value)


def pack_panels(layer, *parts):
    depth = parts[0].shape[1]
    panels = [(i, c) for i, a in enumerate(parts) for c in range(a.shape[2] // TILE)]

    def body(*refs):
        out_ref, sems = refs[-2:]
        copies = [
            pltpu.make_async_copy(
                refs[i].at[layer, :, c * TILE : (c + 1) * TILE], out_ref.at[p], sems.at[p]
            )
            for p, (i, c) in enumerate(panels)
        ]
        start(copies)
        wait(copies)

    return call_once(
        body,
        parts,
        [shape((len(panels), depth, TILE), BF16)],
        [pltpu.SemaphoreType.DMA((len(panels),))],
        hbm=tuple(range(len(parts))),
    )[0]


def turn(x, tables, sign):
    head = x[:, :LANES]
    half = ROT // 2
    up = pltpu.roll(head, LANES - half, 1)
    down = pltpu.roll(head, half, 1)
    head = head * tables[0] + sign * (down * tables[2] - up * tables[1])
    return jnp.concatenate([head, x[:, LANES:]], axis=1)


def add_up(*parts):
    def body(*refs):
        total = refs[0][...].astype(F32)
        for ref in refs[1:-1]:
            total = total + ref[...].astype(F32)
        refs[-1][...] = total.astype(BF16)

    return call_once(body, parts, [shape(parts[0].shape, BF16)])[0]


def add_split(a, b):
    rows, width = a.shape
    n = rows // 4

    def body(a_ref, b_ref, *outs):
        for i, ref in enumerate(outs):
            at = slice(i * n, (i + 1) * n)
            ref[...] = (a_ref[at].astype(F32) + b_ref[at].astype(F32)).astype(BF16)

    return call_once(body, (a, b), [shape((n, width), BF16)] * 4)


def stack_up(*parts):
    n, width = parts[0].shape

    def body(*refs):
        for i, ref in enumerate(refs[:-1]):
            refs[-1][i * n : (i + 1) * n] = ref[...]

    return call_once(body, parts, [shape((n * len(parts), width), BF16)])[0]


def add_late(a, b):
    rows = a.shape[0]

    def body(a_ref, b_ref, out_ref):
        out_ref[...] = (a_ref[...] + b_ref[...].astype(F32)).astype(BF16)

    return call(
        body,
        (1,),
        (a, b),
        [whole(a), pl.BlockSpec((rows, b.shape[1]), lambda *_: (b.shape[0] // rows - 1, 0))],
        [shape(a.shape, BF16)],
        [whole(a)],
    )[0]


def weight_grad(x, ys, blocks, got=None):
    rows, width = x.shape
    cols = [a.shape[1] for a in ys]
    total = sum(cols)
    size = width // 16
    tiles = blocks.shape[0] // 2

    def body(block_ref, x_ref, *rest):
        y_refs = rest[: len(ys)]
        out_ref, xs, sems = rest[-3:]
        j = pl.program_id(0)

        def copy(i):
            at = pl.multiple_of(block_ref[i] * size, size)
            return pltpu.make_async_copy(x_ref.at[:, pl.ds(at, size)], xs.at[i], sems.at[i])

        @pl.when(j == 0)
        def _():
            for i in range(2 * tiles):
                copy(i).start()

        copy(2 * j).wait()
        copy(2 * j + 1).wait()
        left = jnp.concatenate([xs[2 * j], xs[2 * j + 1]], axis=1)
        at = 0
        for ref, n in zip(y_refs, cols):
            y = dot_tn(left, ref[...])
            if got is not None:
                y = y + rest[len(ys)][:, at : at + n].astype(F32)
            out_ref[:, at : at + n] = y.astype(BF16)
            at += n

    ins = (blocks, *pinned(x), *ys)
    specs = [pl.BlockSpec(memory_space=pltpu.HBM)] + [whole(a) for a in ys]
    if got is not None:
        ins += (got,)
        specs += [pl.BlockSpec((2 * size, total), lambda j, *_: (j, 0))]
    return call(
        body,
        (tiles,),
        ins,
        specs,
        [shape((width // 2, total), BF16)],
        [pl.BlockSpec((2 * size, total), lambda j, *_: (j, 0))],
        scratch=[pltpu.VMEM((2 * tiles, rows, size), BF16), pltpu.SemaphoreType.DMA((2 * tiles,))],
        prefetch=1,
        flops=2 * rows * (width // 2) * total,
    )[0]


def scatter_weight_grad(value):
    return lax.psum_scatter(value, "fsdp", scatter_dimension=0, tiled=True)


def swap_half(value):
    return swap_y(value[value.shape[0] // 2 :])


def finish_weight_grads(layers, cols):
    flat = [a for layer in layers for a in layer]
    depth = layers[0][0].shape[0] // 2
    outs = [shape((len(layers), depth, n), F32) for n in cols]

    def body(*refs):
        qkv_ref, dense_ref, up_ref, down_ref = refs[len(flat) :]
        for l in range(len(layers)):
            ins = refs[6 * l : 6 * l + 6]
            out, up, qkv = (
                ins[i][:depth].astype(F32) + ins[3 + i][...].astype(F32) for i in range(3)
            )
            qkv_ref[l] = qkv
            dense_ref[l] = out[:, :HD]
            up_ref[l] = up
            down_ref[l] = out[:, HD:]

    return call_once(body, pinned(*flat), outs)


def body(
    tokens,
    block_order,
    cotangent,
    qkv_weight,
    qkv_bias,
    dense_weight,
    up_weight,
    up_bias,
    down_weight,
    norm_gains,
    norm_shifts,
    out_bias,
):
    seqs, per, width = tokens.shape
    block = 128
    c, t = lax.axis_index("ctx"), lax.axis_index("tp")
    y_hi, z = t // 4, t % 4

    b = jnp.arange(8, dtype=jnp.int32)
    near = (b // 2) * 4 + (c ^ (2 * (b % 2)))
    far = near ^ 1
    row_at = jnp.concatenate(
        [2 * ((z + b // 2) % 4) + b % 2, (y_hi ^ (b // 4)) * 4 + (z + b) % 4]
    )

    row = row_at[:, None] * CHUNK + jnp.arange(CHUNK, dtype=jnp.int32)[None, :]
    row = row.reshape(seqs, per)
    slots = jnp.arange(block_order.shape[0], dtype=jnp.int32)

    def positions(owner):
        slot = 2 * owner + row // block
        here = slot[:, :, None] == slots
        return jnp.sum(jnp.where(here, block_order, 0), axis=2) * block + row % block

    qpos = positions(c).reshape(seqs * per, 1)
    kpos = jnp.concatenate([positions(c ^ i) for i in range(4)], axis=1)
    inverse = 10000.0 ** (-(jnp.arange(ROT // 2, dtype=F32) * 2.0) / ROT)
    angles = qpos.astype(F32) * inverse[None, :]
    cosine, sine = jnp.cos(angles), jnp.sin(angles)
    none = jnp.zeros_like(sine)
    rest = jnp.zeros((seqs * per, LANES - ROT), F32)
    tables = jnp.stack(
        [
            jnp.concatenate([cosine, cosine, rest + 1.0], axis=1),
            jnp.concatenate([sine, none, rest], axis=1),
            jnp.concatenate([none, sine, rest], axis=1),
        ]
    )

    vec = jnp.concatenate(
        [
            norm_gains,
            norm_shifts,
            out_bias[:, None],
            jnp.zeros((LAYERS, 3, width), BF16),
        ],
        axis=1,
    ).astype(F32)
    weights = (qkv_weight, dense_weight, up_weight, down_weight)
    qkv_b = qkv_bias.astype(F32)
    up_b = up_bias.astype(F32)

    kept = []
    rows = seqs * per
    ins = [pack_panels(l, qkv_weight, up_weight) for l in range(1, LAYERS)]
    outs = [pack_panels(l, dense_weight, down_weight) for l in range(1, LAYERS)]
    w = gather_weights(pack_panels(0, *weights))
    w, ins, outs, vec, tables, qpos, kpos, near, far = together(
        w, ins, outs, vec, tables, qpos, kpos, near, far
    )
    w_in, w_out = (w, ALL_PANELS[0], ALL_PANELS[2]), (w, ALL_PANELS[1], ALL_PANELS[3])
    sums = None
    for l in range(LAYERS):
        bias = qkv_b[l : l + 1]
        if l == 0:
            new = first_in(tokens, row_at, vec, w_in, bias, tables)
        else:
            new = next_in(kept[-1][2], sums, l, vec, w_in, bias, tables)
        x, stats, na, nm, q, kv = new
        kv_y, kv_core = swap_y(kv), swap_core(kv)
        active, slope = project_up(nm, w_in, up_b[l : l + 1])
        kv_y, active = together(kv_y, active)
        kvs = [kv, kv_core, kv_y, swap_core(kv_y)]
        mixed, terms = attend_out(q, kvs, qpos, kpos, active, w_out)
        held, moving = tp_1(terms)
        kept.append((w_in, w_out, x, stats, na, nm, q, kvs, mixed, active, slope, terms))
        if l < LAYERS - 1:
            shard, _ = together(ins[l], kv_y)
            w_in = (gather_weights(shard), *IN_PANELS)
            held, moving = tp_2(held, together(*moving))
            shard, moving = together(outs[l], moving)
            (first, second), (firsts, seconds) = tp_3(held, moving)
            seconds, first = together(seconds, first)
            sums = tp_pieces(first, firsts, *tp_4(second, seconds))
            w_out = (gather_weights(shard), *OUT_PANELS)

    late, late_moving = held, moving
    small = [None] * LAYERS
    scattered = [None] * LAYERS
    g = None
    for l in reversed(range(LAYERS)):
        last = l == LAYERS - 1
        w_in, w_out, x, stats, na, nm, q, kvs, mixed, active, slope, terms = kept[l]
        if last:
            slope, _ = together(slope, terms)
            g, gm, gh, part = last_back_out(cotangent, row_at, w_out, slope)
            late_moving, gm = together(late_moving, gm)
            late, late_moving = tp_2(late, late_moving)
        else:
            after = kept[l + 1]
            g, gm, gh, part = next_back_out(g, after[2], after[3], sums, w_out, slope)
        dq, own, to_y, send = attend_back(q, kvs, gm, qpos, kpos)
        from_core = swap_core(send)
        out_far = weight_grad(g, pinned(mixed, active), far)
        if last:
            late_moving, out_far = together(late_moving, out_far)
        else:
            late_first, late_second = tp_3_sums(late, late_moving)
            late_seconds = [from_z(late_second, k) for k in (1, 3, 2)]
            late_seconds, out_far = together(late_seconds, out_far)
            late_near, late_far = tp_4(late_second, late_seconds)
            late_firsts = [from_z(late_first, k) for k in (1, 3, 2)]
        from_core, out_far = together(from_core, out_far)
        from_y = swap_y(add_late(to_y, from_core))
        out_got = swap_core(out_far)
        up_far = weight_grad(nm, pinned(gh), far)
        if last:
            out_got, up_far = together(out_got, up_far)
        else:
            out_got, up_far, late_far = together(out_got, up_far, late_far)
        out_near = weight_grad(g, pinned(mixed, active), near, out_got)
        up_got, out_near = together(swap_core(up_far), out_near)
        up_near = weight_grad(nm, pinned(gh), near, up_got)
        if last:
            from_y, out_near, up_near = together(from_y, out_near, up_near)
        else:
            out_after, up_after, qkv_after = scattered[l + 1]
            from_y, out_near, up_near, qkv_after = together(from_y, out_near, up_near, qkv_after)
            out_half, up_half = swap_half(out_after), swap_half(up_after)
        out_sum = scatter_weight_grad(out_near)
        gp, terms, small[l] = back_in(
            dq, own, from_core, from_y, tables, gh, w_in, x, stats, vec, l, part
        )
        if not last:
            late_firsts, out_half, up_half, gp = together(late_firsts, out_half, up_half, gp)
        held, moving = tp_1(terms)
        up_sum = scatter_weight_grad(up_near)
        qkv_far = weight_grad(na, (gp,), far)
        moving, qkv_far, out_sum = together(moving, qkv_far, out_sum)
        held, moving = tp_2(held, moving)
        qkv_got = swap_core(qkv_far)
        if last:
            moving, qkv_got = together(moving, qkv_got)
        else:
            total = jnp.stack(small)
            parts = around_ctx(total)
            moving, qkv_got, parts = together(moving, qkv_got, parts)
        first, second = tp_3_sums(held, moving)
        second, first, qkv_got = together(second, first, qkv_got)
        seconds = [from_z(second, k) for k in (1, 3, 2)]
        firsts = [from_z(first, k) for k in (1, 3, 2)]
        qkv_near = weight_grad(na, (gp,), near, qkv_got)
        qkv_sum = scatter_weight_grad(qkv_near)
        if last:
            seconds, qkv_near, up_sum = together(seconds, qkv_near, up_sum)
            sums = tp_pieces(first, firsts, *tp_4(second, seconds))
        else:
            total = pair_up(total, parts)
            parts = around(total, from_x)
            qkv_half, next_half = swap_half(qkv_after), swap_half(out_sum)
            seconds, qkv_near, parts, qkv_half, next_half = together(
                seconds, qkv_near, parts, qkv_half, next_half
            )
            halves = [[next_half], [out_half, up_half, qkv_half]]
            scattered[l + 1] = (out_after, up_after, qkv_after)
            sum_near, sum_far = tp_4(second, seconds)
            total = pair_up(total, parts)
            wide = total[:, :4]
            parts = around(wide, from_z)
            late_pieces = tp_pieces(late_first, late_firsts, late_near, late_far)
            activations = last_stream(tokens, row_at, kept[-1][2], late_pieces, vec, LAYERS - 1)
            sum_far, firsts, parts, activations = together(sum_far, firsts, parts, activations)
            halves[0] += [swap_half(up_sum), swap_half(qkv_sum)]
            wide = pair_up(wide, parts)
            wide = wide + swap_tp(wide, 4)
            sums = tp_pieces(first, firsts, sum_near, sum_far)
        scattered[l] = (out_sum, up_sum, qkv_sum)
    input_grad = last_grad(tokens, row_at, g, kept[0][2], kept[0][3], sums)
    input_grad, halves = together(input_grad, halves)
    qkv_grad, dense_grad, up_grad, down_grad = finish_weight_grads(
        [(*scattered[l], *halves[l]) for l in range(LAYERS)],
        [a.shape[2] for a in weights],
    )
    return (
        activations,
        input_grad,
        qkv_grad,
        total[:, 5, : qkv_bias.shape[1]],
        dense_grad,
        up_grad,
        total[:, 6, : up_bias.shape[1]],
        down_grad,
        wide[:, 0:2],
        wide[:, 2:4],
        total[:, 4],
    )


def solution(mesh):
    weight = P(None, ("fsdp", "ctx"), "tp")
    stream = P("fsdp", "ctx", None)
    bias = P(None, "tp")
    return jax.shard_map(
        body,
        mesh=mesh,
        in_specs=(
            stream,
            P(),
            stream,
            weight,
            bias,
            weight,
            weight,
            bias,
            weight,
            P(),
            P(),
            P(),
        ),
        out_specs=(
            stream,
            stream,
            weight,
            bias,
            weight,
            weight,
            bias,
            weight,
            P(),
            P(),
            P(),
        ),
        check_vma=False,
    )
```

profile of v0, /device:TPU:0, one launch (start us, length us, event | category | flops | bytes accessed | tf_op | source)
XLA Modules:
  0.0 590.1 jit_solution(9595009530938007875)
XLA Ops:
  16.8 67.7 %all-gather.4.cloned.1.call-done.w_ref.rest_6_ = bf16[12,2048,256]{2,1,0:T(8,128)(2,1)} async-done(((bf16[12,128,256]{2,1,0:T(8,128)(2,1)}), bf16[12,2048,256]{2,1,0:T(8,128)(2,1)}) %all-gather.4.cloned.1.call-update) | async-done | bytes 12582928 | tf_op jit(solution)/shard_map/all_gather | solution.py:51
  84.6 9.2 %shard_map.206 = (bf16[512,2048]{1,0:T(8,128)(2,1)S(1)}, f32[512,128]{1,0:T(8,128)S(1)}, bf16[512,2048]{1,0:T(8,128)(2,1)S(1)}, bf16[512,2048]{1,0:T(8,128)(2,1)...) custom-call(s32[16]{0:T(128)S(1)} %pad_add_fusion.1.row_ref, bf16[2,256,2048]{2,1,0:T(8,128)(2,1)} %tok_ref.1, ...), custom_call_target="tpu_custom_call" | custom-call | flops 1610612736 | bytes 14552128 | tf_op jit(solution)/shard_map/pallas_call | solution.py:108
  98.0 7.6 %shard_map.207 = (bf16[512,1024]{1,0:T(8,128)(2,1)S(1)}, bf16[512,1024]{1,0:T(8,128)(2,1)S(1)}) custom-call(bf16[512,2048]{1,0:T(8,128)(2,1)S(1)} %get-tuple-element.224.n_ref.x_ref, bf16[12,2048,256]{2,1,0:T(8,128)(2,1)} %all-gather.4.cloned.1.call-done.w_ref.rest_6_, f32[1,1024]{1,0:T(1,128)S(1)} %get-tuple-element.440.b_ref), custom_call_target="tpu_custom_call" | custom-call | flops 2147483648 | bytes 8392704 | tf_op jit(solution)/shard_map/pallas_call | solution.py:108
  107.6 3.0 collective-permute-done.1.k2
  114.9 6.6 %shard_map.208 = (bf16[512,256]{1,0:T(8,128)(2,1)S(1)}, bf16[64,2048]{1,0:T(8,128)(2,1)S(1)}, bf16[64,2048]{1,0:T(8,128)(2,1)S(1)}, bf16[64,2048]{1,0:T(8,128)(2...) custom-call(bf16[512,256]{1,0:T(8,128)(2,1)S(1)} %get-tuple-element.222.q_ref, ...), custom_call_target="tpu_custom_call" | custom-call | flops 3221225472 | bytes 9971712 | tf_op jit(solution)/shard_map/pallas_call | solution.py:108
  122.2 2.9 collective-permute-start.6
  130.5 4.1 collective-permute-done.3.refs_1_
  134.6 5.0 collective-permute-done.4.refs_2_
  141.4 8.0 %collective-permute-done.6.b_ref = bf16[128,2048]{1,0:T(8,128)(2,1)S(1)} collective-permute-done((bf16[128,2048]{1,0:T(8,128)(2,1)S(1)}, bf16[128,2048]{1,0:T(8,128)(2,1)S(1)}, u32[]{:S(2)}, u32[]{:S(2)}) %collective-permute-start.6) | collective-permute-done | bytes 524320 | tf_op jit(solution)/shard_map/ppermute | solution.py:39
  149.6 2.9 collective-permute-start.7
  160.4 2.4 collective-permute-done.10.refs_3_
  162.8 2.6 collective-permute-done.7.refs_1_
  165.5 3.0 collective-permute-start.11
  172.4 3.7 collective-permute-done.12.refs_3_
  176.2 2.9 collective-permute-start.17
  182.1 7.1 %collective-permute-done.14.rest_1_ = bf16[64,2048]{1,0:T(8,128)(2,1)S(1)} collective-permute-done((bf16[64,2048]{1,0:T(8,128)(2,1)S(1)}, bf16[64,2048]{1,0:T(8,128)(2,1)S(1)}, u32[]{:S(2)}, u32[]{:S(2)}) %collective-permute-start.14) | collective-permute-done | bytes 262176 | tf_op jit(solution)/shard_map/ppermute | solution.py:43
  190.2 2.7 collective-permute-done.16.rest_3_
  193.7 9.2 %shard_map.214 = (bf16[512,2048]{1,0:T(8,128)(2,1)S(1)}, f32[512,128]{1,0:T(8,128)S(1)}, bf16[512,2048]{1,0:T(8,128)(2,1)S(1)}, bf16[512,2048]{1,0:T(8,128)(2,1)...) custom-call(bf16[512,2048]{1,0:T(8,128)(2,1)} %copy-done.3, bf16[64,2048]{1,0:T(8,128)(2,1)} %copy-done.34, ...), custom_call_target="tpu_custom_call" | custom-call | flops 1610612736 | bytes 16649216 | tf_op jit(solution)/shard_map/pallas_call | solution.py:108
  207.4 7.6 %shard_map.215 = (bf16[512,1024]{1,0:T(8,128)(2,1)S(1)}, bf16[512,1024]{1,0:T(8,128)(2,1)S(1)}) custom-call(bf16[512,2048]{1,0:T(8,128)(2,1)S(1)} %get-tuple-element.257.n_ref.x_ref, bf16[7,2048,256]{2,1,0:T(8,128)(2,1)} %all-gather.8.cloned.1.call-done.rest_7_.w_ref, f32[1,1024]{1,0:T(1,128)S(1)} %get-tuple-element.439.b_ref), custom_call_target="tpu_custom_call" | custom-call | flops 2147483648 | bytes 8392704 | tf_op jit(solution)/shard_map/pallas_call | solution.py:108
  216.9 9.2 %collective-permute-done.19.k2 = bf16[512,512]{1,0:T(8,128)(2,1)S(1)} collective-permute-done((bf16[512,512]{1,0:T(8,128)(2,1)S(1)}, bf16[512,512]{1,0:T(8,128)(2,1)S(1)}, u32[]{:S(2)}, u32[]{:S(2)}) %collective-permute-start.19) | collective-permute-done | bytes 524320 | tf_op jit(solution)/shard_map/ppermute | solution.py:27
  229.4 7.6 %shard_map.216 = (bf16[512,256]{1,0:T(8,128)(2,1)S(1)}, bf16[64,2048]{1,0:T(8,128)(2,1)S(1)}, bf16[64,2048]{1,0:T(8,128)(2,1)S(1)}, bf16[64,2048]{1,0:T(8,128)(2...) custom-call(bf16[512,256]{1,0:T(8,128)(2,1)S(1)} %copy-done.94, ...), custom_call_target="tpu_custom_call" | custom-call | flops 3221225472 | bytes 9971712 | tf_op jit(solution)/shard_map/pallas_call | solution.py:108
  237.0 2.9 collective-permute-start.24
  245.2 10.5 %shard_map.217 = (bf16[512,2048]{1,0:T(8,128)(2,1)S(1)}, bf16[512,256]{1,0:T(8,128)(2,1)S(1)}, bf16[512,1024]{1,0:T(8,128)(2,1)S(1)}, f32[8,2048]{1,0:T(8,128)S(1)}) custom-call(s32[16]{0:T(128)S(1)} %pad_add_fusion.1.row_ref, bf16[2,256,2048]{2,1,0:T(8,128)(2,1)} %cot_ref.1, bf16[5,2048,256]{2,1,0:T(8,128)(2,1)} %all-gather.6.cloned.1.call-done.w_ref, ...), custom_call_target="tpu_custom_call" | custom-call | flops 2684354560 | bytes 10813504 | tf_op jit(solution)/shard_map/pallas_call | solution.py:108
  258.1 4.0 shard_map.218
  265.0 2.6 collective-permute-start.28
  267.9 5.2 shard_map.221
  275.9 5.9 %shard_map.223 = bf16[1024,1024]{1,0:T(8,128)(2,1)} custom-call(s32[8]{0:T(128)S(1)} %get-tuple-element.286.block_ref, bf16[512,2048]{1,0:T(8,128)(2,1)} %copy-done.5, bf16[512,1024]{1,0:T(8,128)(2,1)} %copy-done.6), custom_call_target="tpu_custom_call" | custom-call | flops 1073741824 | bytes 5242912 | tf_op jit(solution)/shard_map/pallas_call | solution.py:108
  283.6 6.3 %shard_map.224 = bf16[1024,1280]{1,0:T(8,128)(2,1)} custom-call(s32[8]{0:T(128)S(1)} %get-tuple-element.294.block_ref, bf16[512,2048]{1,0:T(8,128)(2,1)} %copy-done, bf16[512,256]{1,0:T(8,128)(2,1)} %copy-done.33, bf16[512,1024]{1,0:T(8,128)(2,1)} %copy-done.14, bf16[1024,1280]{1,0:T(8,128)(2,1)S(1)} %collective-permute-done.31.rest_2_), custom_call_target="tpu_custom_call" | custom-call | flops 1342177280 | bytes 8650784 | tf_op jit(solution)/shard_map/pallas_call | solution.py:108
  289.9 6.7 %shard_map.225 = bf16[1024,1024]{1,0:T(8,128)(2,1)} custom-call(s32[8]{0:T(128)S(1)} %get-tuple-element.294.block_ref, bf16[512,2048]{1,0:T(8,128)(2,1)} %copy-done.5, bf16[512,1024]{1,0:T(8,128)(2,1)} %copy-done.6, bf16[1024,1024]{1,0:T(8,128)(2,1)} %collective-permute-done.32.rest_1_), custom_call_target="tpu_custom_call" | custom-call | flops 1073741824 | bytes 7340064 | tf_op jit(solution)/shard_map/pallas_call | solution.py:108
  297.5 12.6 %shard_map.226 = (bf16[512,768]{1,0:T(8,128)(2,1)S(1)}, bf16[64,2048]{1,0:T(8,128)(2,1)S(1)}, bf16[64,2048]{1,0:T(8,128)(2,1)S(1)}, bf16[64,2048]{1,0:T(8,128)(2...) custom-call(f32[512,256]{1,0:T(8,128)} %copy-done.40, ...), custom_call_target="tpu_custom_call" | custom-call | flops 3758096384 | bytes 14680064 | tf_op jit(solution)/shard_map/pallas_call | solution.py:108
  311.4 2.7 collective-permute-start.36
  314.5 2.8 collective-permute-start.34
  319.2 3.4 shard_map.227
  324.1 3.8 collective-permute-done.34.refs_2_
  354.4 4.5 shard_map.232
  358.8 3.5 reduce-scatter.9.cloned.1.call-done.refs_7_
  362.4 3.1 collective-permute-start.48
  365.4 3.0 collective-permute-start.42
  370.4 8.9 %collective-permute-done.42.rest_1_ = bf16[64,2048]{1,0:T(8,128)(2,1)S(1)} collective-permute-done((bf16[64,2048]{1,0:T(8,128)(2,1)S(1)}, bf16[64,2048]{1,0:T(8,128)(2,1)S(1)}, u32[]{:S(2)}, u32[]{:S(2)}) %collective-permute-start.42) | collective-permute-done | bytes 262176 | tf_op jit(solution)/shard_map/ppermute | solution.py:43
  379.4 3.7 collective-permute-done.44.rest_3_
  383.9 12.2 %shard_map.234 = (bf16[512,2048]{1,0:T(8,128)(2,1)S(1)}, bf16[512,256]{1,0:T(8,128)(2,1)S(1)}, bf16[512,1024]{1,0:T(8,128)(2,1)S(1)}, f32[8,2048]{1,0:T(8,128)S(1)}) custom-call(bf16[512,2048]{1,0:T(8,128)(2,1)} %copy-done, bf16[512,2048]{1,0:T(8,128)(2,1)} %copy-done.1, f32[512,128]{1,0:T(8,128)S(1)} %get-tuple-element.273.stat_ref, ...), custom_call_target="tpu_custom_call" | custom-call | flops 2684354560 | bytes 15269888 | tf_op jit(solution)/shard_map/pallas_call | solution.py:108
  399.1 4.0 shard_map.235
  406.9 6.3 %shard_map.237 = bf16[1024,1280]{1,0:T(8,128)(2,1)} custom-call(s32[8]{0:T(128)S(1)} %get-tuple-element.286.block_ref, bf16[512,2048]{1,0:T(8,128)(2,1)} %copy-done.2, bf16[512,256]{1,0:T(8,128)(2,1)} %copy-done.28, bf16[512,1024]{1,0:T(8,128)(2,1)} %copy-done.7), custom_call_target="tpu_custom_call" | custom-call | flops 1342177280 | bytes 6029344 | tf_op jit(solution)/shard_map/pallas_call | solution.py:108
  415.3 5.8 shard_map.239
  421.1 9.5 %collective-permute-done.55.rest_6_ = bf16[128,2048]{1,0:T(8,128)(2,1)S(1)} collective-permute-done((bf16[128,2048]{1,0:T(8,128)(2,1)S(1)}, bf16[128,2048]{1,0:T(8,128)(2,1)S(1)}, u32[]{:S(2)}, u32[]{:S(2)}) %collective-permute-start.55) | collective-permute-done | bytes 524320 | tf_op jit(solution)/shard_map/ppermute | solution.py:39
  432.2 7.1 %shard_map.241 = bf16[1024,1280]{1,0:T(8,128)(2,1)} custom-call(s32[8]{0:T(128)S(1)} %get-tuple-element.294.block_ref, bf16[512,2048]{1,0:T(8,128)(2,1)} %copy-done.2, bf16[512,256]{1,0:T(8,128)(2,1)} %copy-done.28, bf16[512,1024]{1,0:T(8,128)(2,1)} %copy-done.7, bf16[1024,1280]{1,0:T(8,128)(2,1)} %collective-permute-done.54.rest_2_), custom_call_target="tpu_custom_call" | custom-call | flops 1342177280 | bytes 8650784 | tf_op jit(solution)/shard_map/pallas_call | solution.py:108
  439.2 6.6 %shard_map.242 = bf16[1024,1024]{1,0:T(8,128)(2,1)} custom-call(s32[8]{0:T(128)S(1)} %get-tuple-element.294.block_ref, bf16[512,2048]{1,0:T(8,128)(2,1)} %copy-done.4, bf16[512,1024]{1,0:T(8,128)(2,1)} %copy-done.9, bf16[1024,1024]{1,0:T(8,128)(2,1)} %collective-permute-done.56.rest_1_), custom_call_target="tpu_custom_call" | custom-call | flops 1073741824 | bytes 7340064 | tf_op jit(solution)/shard_map/pallas_call | solution.py:108
  452.5 12.7 %shard_map.243 = (bf16[512,768]{1,0:T(8,128)(2,1)S(1)}, bf16[64,2048]{1,0:T(8,128)(2,1)S(1)}, bf16[64,2048]{1,0:T(8,128)(2,1)S(1)}, bf16[64,2048]{1,0:T(8,128)(2...) custom-call(f32[512,256]{1,0:T(8,128)} %copy-done.39, ...), custom_call_target="tpu_custom_call" | custom-call | flops 3758096384 | bytes 14680064 | tf_op jit(solution)/shard_map/pallas_call | solution.py:108
  472.0 11.7 %collective-permute-done.65.refs_10_ = bf16[128,1024]{1,0:T(8,128)(2,1)S(1)} collective-permute-done((bf16[128,1024]{1,0:T(8,128)(2,1)S(1)}, bf16[128,1024]{1,0:T(8,128)(2,1)S(1)}, u32[]{:S(2)}, u32[]{:S(2)}) %collective-permute-start.65) | collective-permute-done | bytes 262176 | tf_op jit(solution)/shard_map/ppermute | solution.py:27
  483.7 3.3 shard_map.245
  496.2 3.0 collective-permute-start.66
  505.1 2.9 collective-permute-done.67.refs_1_
  511.4 4.4 shard_map.250
  518.1 2.6 collective-permute-start.74
  524.4 3.6 collective-permute-done.81.refs_3_
  529.5 2.8 collective-permute-start.83
  533.9 5.0 collective-permute-done.78
  541.1 3.1 collective-permute-start.86
  548.5 3.4 collective-permute-done.87
  553.9 4.7 shard_map.252
  559.5 2.5 collective-permute-start.91
  565.6 6.3 %shard_map.253 = f32[2,256,2048]{2,1,0:T(8,128)} custom-call(s32[16]{0:T(128)S(1)} %copy-done.88, bf16[512,2048]{1,0:T(8,128)(2,1)} %copy-done.2, bf16[512,2048]{1,0:T(8,128)(2,1)} %copy-done.3, bf16[64,2048]{1,0:T(8,128)(2,1)} %copy-done.32, bf16[64,2048]{1,0:T(8,128)(2,1)} %copy-done.112, bf16[64,2048]{1,0:T(8,128)(2,1)} %copy-done.114, ...), custom_call_target="tpu_custom_call" | custom-call | bytes 10747968 | tf_op jit(solution)/shard_map/pallas_call | solution.py:108
  575.0 3.6 collective-permute-done.90.refs_5_
  579.3 4.1 shard_map.254
  (524 shorter events, 172.5 us)
Async XLA Ops:
  7.2 77.4 %all-gather.4.cloned.1.call-start = ((), (), s32[]{:S(2)}) async-start(), calls=%async_computation.6 | async-start | bytes 13369344 | tf_op jit(solution)/shard_map/all_gather | solution.py:51
  9.4 183.4 %all-gather.8.cloned.1.call-start = ((), (), s32[]{:S(2)}) async-start(), calls=%async_computation.8 | async-start | bytes 7798784 | tf_op jit(solution)/shard_map/all_gather | solution.py:51
  96.5 14.2 %collective-permute-start.1 = (bf16[512,512]{1,0:T(8,128)(2,1)S(1)}, bf16[512,512]{1,0:T(8,128)(2,1)S(1)}, u32[]{:S(2)}, u32[]{:S(2)}) collective-permute-start(bf16[512,512]{1,0:T(8,128)(2,1)S(1)} %get-tuple-element.223.k0), channel_id=1, source_target_pairs={{0,16},{8,24},{16,0},{24,8},{1,17},{9,25},{17,1},{25,9},{2,18},{10... | collective-permute-start | bytes 1572872 | tf_op jit(solution)/shard_map/ppermute | solution.py:27
  110.7 115.5 %all-gather.6.cloned.1.call-start = ((), (), s32[]{:S(2)}) async-start(), calls=%async_computation.7 | async-start | bytes 5570560 | tf_op jit(solution)/shard_map/all_gather | solution.py:51
  122.2 27.2 %collective-permute-start.6 = (bf16[128,2048]{1,0:T(8,128)(2,1)S(1)}, bf16[128,2048]{1,0:T(8,128)(2,1)S(1)}, u32[]{:S(2)}, u32[]{:S(2)}) collective-permute-start(bf16[128,2048]{1,0:T(8,128)(2,1)S(1)} %get-tuple-element.235), channel_id=1, source_target_pairs={{0,4},{1,5},{2,6},{3,7},{4,0},{5,1},{6,2},{7,3},{8,12},{9,13},{10,... | collective-permute-start | bytes 1572872 | tf_op jit(solution)/shard_map/ppermute | solution.py:39
  126.8 12.8 %collective-permute-start.4 = (bf16[64,2048]{1,0:T(8,128)(2,1)S(1)}, bf16[64,2048]{1,0:T(8,128)(2,1)S(1)}, u32[]{:S(2)}, u32[]{:S(2)}) collective-permute-start(bf16[64,2048]{1,0:T(8,128)(2,1)S(1)} %get-tuple-element.233), channel_id=1, source_target_pairs={{0,3},{1,0},{2,1},{3,2},{4,7},{5,4},{6,5},{7,6},{8,11},{9,8},{10,9... | collective-permute-start | bytes 786440 | tf_op jit(solution)/shard_map/ppermute | solution.py:47
  128.5 12.9 %collective-permute-start.5 = (bf16[64,2048]{1,0:T(8,128)(2,1)S(1)}, bf16[64,2048]{1,0:T(8,128)(2,1)S(1)}, u32[]{:S(2)}, u32[]{:S(2)}) collective-permute-start(bf16[64,2048]{1,0:T(8,128)(2,1)S(1)} %get-tuple-element.234), channel_id=1, source_target_pairs={{0,2},{1,3},{2,0},{3,1},{4,6},{5,7},{6,4},{7,5},{8,10},{9,11},{10,... | collective-permute-start | bytes 786440 | tf_op jit(solution)/shard_map/ppermute | solution.py:47
  149.6 15.8 %collective-permute-start.7 = (bf16[64,2048]{1,0:T(8,128)(2,1)S(1)}, bf16[64,2048]{1,0:T(8,128)(2,1)S(1)}, u32[]{:S(2)}, u32[]{:S(2)}) collective-permute-start(bf16[64,2048]{1,0:T(8,128)(2,1)S(1)} %shard_map.209.refs_0_), channel_id=1, source_target_pairs={{0,4},{1,5},{2,6},{3,7},{4,0},{5,1},{6,2},{7,3},{8,12},{9,13},{10,... | collective-permute-start | bytes 786440 | tf_op jit(solution)/shard_map/ppermute | solution.py:39
  165.4 166.0 %reduce-scatter.7.cloned.1.call-start = ((), (), s32[]{:S(2)}) async-start(), calls=%async_computation.9 | async-start | bytes 3276800 | tf_op jit(solution)/shard_map/reduce_scatter | solution.py:896
  176.2 16.7 %collective-permute-start.17 = (bf16[128,2048]{1,0:T(8,128)(2,1)S(1)}, bf16[128,2048]{1,0:T(8,128)(2,1)S(1)}, u32[]{:S(2)}, u32[]{:S(2)}) collective-permute-start(bf16[128,2048]{1,0:T(8,128)(2,1)S(1)} %shard_map.213.rest_4_), channel_id=1, source_target_pairs={{0,4},{1,5},{2,6},{3,7},{4,0},{5,1},{6,2},{7,3},{8,12},{9,13},{10,... | collective-permute-start | bytes 1572872 | tf_op jit(solution)/shard_map/ppermute | solution.py:39
  181.2 11.6 %collective-permute-start.16 = (bf16[64,2048]{1,0:T(8,128)(2,1)S(1)}, bf16[64,2048]{1,0:T(8,128)(2,1)S(1)}, u32[]{:S(2)}, u32[]{:S(2)}) collective-permute-start(bf16[64,2048]{1,0:T(8,128)(2,1)S(1)} %shard_map.212.rest_0_), channel_id=1, source_target_pairs={{3,0},{0,1},{1,2},{2,3},{7,4},{4,5},{5,6},{6,7},{11,8},{8,9},{9,10... | collective-permute-start | bytes 786440 | tf_op jit(solution)/shard_map/ppermute | solution.py:43
  206.2 19.9 %collective-permute-start.19 = (bf16[512,512]{1,0:T(8,128)(2,1)S(1)}, bf16[512,512]{1,0:T(8,128)(2,1)S(1)}, u32[]{:S(2)}, u32[]{:S(2)}) collective-permute-start(bf16[512,512]{1,0:T(8,128)(2,1)S(1)} %get-tuple-element.260.k0), channel_id=1, source_target_pairs={{0,16},{8,24},{16,0},{24,8},{1,17},{9,25},{17,1},{25,9},{2,18},{10... | collective-permute-start | bytes 1572872 | tf_op jit(solution)/shard_map/ppermute | solution.py:27
  206.9 19.2 %collective-permute-start.18 = (bf16[512,512]{1,0:T(8,128)(2,1)S(1)}, bf16[512,512]{1,0:T(8,128)(2,1)S(1)}, u32[]{:S(2)}, u32[]{:S(2)}) collective-permute-start(bf16[512,512]{1,0:T(8,128)(2,1)S(1)} %get-tuple-element.260.k0), channel_id=1, source_target_pairs={{0,8},{8,0},{16,24},{24,16},{1,9},{9,1},{17,25},{25,17},{2,10},{10... | collective-permute-start | bytes 1572872 | tf_op jit(solution)/shard_map/ppermute | solution.py:23
  237.0 21.1 %collective-permute-start.24 = (bf16[128,2048]{1,0:T(8,128)(2,1)S(1)}, bf16[128,2048]{1,0:T(8,128)(2,1)S(1)}, u32[]{:S(2)}, u32[]{:S(2)}) collective-permute-start(bf16[128,2048]{1,0:T(8,128)(2,1)S(1)} %get-tuple-element.269), channel_id=1, source_target_pairs={{0,4},{1,5},{2,6},{3,7},{4,0},{5,1},{6,2},{7,3},{8,12},{9,13},{10,... | collective-permute-start | bytes 1572872 | tf_op jit(solution)/shard_map/ppermute | solution.py:39
  239.9 18.2 %collective-permute-start.21 = (bf16[64,2048]{1,0:T(8,128)(2,1)S(1)}, bf16[64,2048]{1,0:T(8,128)(2,1)S(1)}, u32[]{:S(2)}, u32[]{:S(2)}) collective-permute-start(bf16[64,2048]{1,0:T(8,128)(2,1)S(1)} %get-tuple-element.265), channel_id=1, source_target_pairs={{0,1},{1,2},{2,3},{3,0},{4,5},{5,6},{6,7},{7,4},{8,9},{9,10},{10,1... | collective-permute-start | bytes 786440 | tf_op jit(solution)/shard_map/ppermute | solution.py:47
  241.4 16.7 %collective-permute-start.22 = (bf16[64,2048]{1,0:T(8,128)(2,1)S(1)}, bf16[64,2048]{1,0:T(8,128)(2,1)S(1)}, u32[]{:S(2)}, u32[]{:S(2)}) collective-permute-start(bf16[64,2048]{1,0:T(8,128)(2,1)S(1)} %get-tuple-element.267), channel_id=1, source_target_pairs={{0,3},{1,0},{2,1},{3,2},{4,7},{5,4},{6,5},{7,6},{8,11},{9,8},{10,9... | collective-permute-start | bytes 786440 | tf_op jit(solution)/shard_map/ppermute | solution.py:47
  243.1 14.9 %collective-permute-start.23 = (bf16[64,2048]{1,0:T(8,128)(2,1)S(1)}, bf16[64,2048]{1,0:T(8,128)(2,1)S(1)}, u32[]{:S(2)}, u32[]{:S(2)}) collective-permute-start(bf16[64,2048]{1,0:T(8,128)(2,1)S(1)} %get-tuple-element.266), channel_id=1, source_target_pairs={{0,2},{1,3},{2,0},{3,1},{4,6},{5,7},{6,4},{7,5},{8,10},{9,11},{10,... | collective-permute-start | bytes 786440 | tf_op jit(solution)/shard_map/ppermute | solution.py:47
  263.1 12.8 %collective-permute-start.25 = (bf16[1024,512]{1,0:T(8,128)(2,1)S(1)}, bf16[1024,512]{1,0:T(8,128)(2,1)S(1)}, u32[]{:S(2)}, u32[]{:S(2)}) collective-permute-start(bf16[1024,512]{1,0:T(8,128)(2,1)S(1)} %get-tuple-element.278), channel_id=1, source_target_pairs={{0,8},{8,0},{16,24},{24,16},{1,9},{9,1},{17,25},{25,17},{2,10},{10... | collective-permute-start | bytes 3145736 | tf_op jit(solution)/shard_map/ppermute | solution.py:23
  263.3 11.9 %collective-permute-start.26 = (bf16[64,2048]{1,0:T(8,128)(2,1)S(1)}, bf16[64,2048]{1,0:T(8,128)(2,1)S(1)}, u32[]{:S(2)}, u32[]{:S(2)}) collective-permute-start(bf16[64,2048]{1,0:T(8,128)(2,1)S(1)} %shard_map.219.refs_0_), channel_id=1, source_target_pairs={{0,4},{1,5},{2,6},{3,7},{4,0},{5,1},{6,2},{7,3},{8,12},{9,13},{10,... | collective-permute-start | bytes 786440 | tf_op jit(solution)/shard_map/ppermute | solution.py:39
  282.5 14.1 %collective-permute-start.30 = (bf16[512,512]{1,0:T(8,128)(2,1)S(1)}, bf16[512,512]{1,0:T(8,128)(2,1)S(1)}, u32[]{:S(2)}, u32[]{:S(2)}) collective-permute-start(bf16[512,512]{1,0:T(8,128)(2,1)S(1)} %shard_map.222), channel_id=1, source_target_pairs={{0,16},{8,24},{16,0},{24,8},{1,17},{9,25},{17,1},{25,9},{2,18},{10... | collective-permute-start | bytes 1572872 | tf_op jit(solution)/shard_map/ppermute | solution.py:27
  296.7 65.6 %reduce-scatter.9.cloned.1.call-start = ((), (), s32[]{:S(2)}) async-start(), calls=%async_computation.10 | async-start | bytes 2621440 | tf_op jit(solution)/shard_map/reduce_scatter | solution.py:896
  297.2 148.6 %reduce-scatter.11.cloned.1.call-start = ((), (), s32[]{:S(2)}) async-start(), calls=%async_computation.11 | async-start | bytes 1966080 | tf_op jit(solution)/shard_map/reduce_scatter | solution.py:896
  311.4 19.1 %collective-permute-start.36 = (bf16[128,2048]{1,0:T(8,128)(2,1)S(1)}, bf16[128,2048]{1,0:T(8,128)(2,1)S(1)}, u32[]{:S(2)}, u32[]{:S(2)}) collective-permute-start(bf16[128,2048]{1,0:T(8,128)(2,1)S(1)} %get-tuple-element.304), channel_id=1, source_target_pairs={{0,4},{1,5},{2,6},{3,7},{4,0},{5,1},{6,2},{7,3},{8,12},{9,13},{10,... | collective-permute-start | bytes 1572872 | tf_op jit(solution)/shard_map/ppermute | solution.py:39
  314.5 13.4 %collective-permute-start.34 = (bf16[64,2048]{1,0:T(8,128)(2,1)S(1)}, bf16[64,2048]{1,0:T(8,128)(2,1)S(1)}, u32[]{:S(2)}, u32[]{:S(2)}) collective-permute-start(bf16[64,2048]{1,0:T(8,128)(2,1)S(1)} %get-tuple-element.302), channel_id=1, source_target_pairs={{0,3},{1,0},{2,1},{3,2},{4,7},{5,4},{6,5},{7,6},{8,11},{9,8},{10,9... | collective-permute-start | bytes 786440 | tf_op jit(solution)/shard_map/ppermute | solution.py:47
  317.3 12.5 %collective-permute-start.35 = (bf16[64,2048]{1,0:T(8,128)(2,1)S(1)}, bf16[64,2048]{1,0:T(8,128)(2,1)S(1)}, u32[]{:S(2)}, u32[]{:S(2)}) collective-permute-start(bf16[64,2048]{1,0:T(8,128)(2,1)S(1)} %get-tuple-element.303), channel_id=1, source_target_pairs={{0,2},{1,3},{2,0},{3,1},{4,6},{5,7},{6,4},{7,5},{8,10},{9,11},{10,... | collective-permute-start | bytes 786440 | tf_op jit(solution)/shard_map/ppermute | solution.py:47
  331.4 19.4 %collective-permute-start.41 = (bf16[1024,768]{1,0:T(8,128)(2,1)S(1)}, bf16[1024,768]{1,0:T(8,128)(2,1)S(1)}, u32[]{:S(2)}, u32[]{:S(2)}) collective-permute-start(bf16[1024,768]{1,0:T(8,128)(2,1)S(1)} %shard_map.227), channel_id=1, source_target_pairs={{0,8},{8,0},{16,24},{24,16},{1,9},{9,1},{17,25},{25,17},{2,10},{10... | collective-permute-start | bytes 4718600 | tf_op jit(solution)/shard_map/ppermute | solution.py:23
  335.3 15.4 %collective-permute-start.37 = (bf16[64,2048]{1,0:T(8,128)(2,1)S(1)}, bf16[64,2048]{1,0:T(8,128)(2,1)S(1)}, u32[]{:S(2)}, u32[]{:S(2)}) collective-permute-start(bf16[64,2048]{1,0:T(8,128)(2,1)S(1)} %shard_map.229.refs_0_), channel_id=1, source_target_pairs={{0,4},{1,5},{2,6},{3,7},{4,0},{5,1},{6,2},{7,3},{8,12},{9,13},{10,... | collective-permute-start | bytes 786440 | tf_op jit(solution)/shard_map/ppermute | solution.py:39
  350.9 11.4 %collective-permute-start.45 = (bf16[32,2048]{1,0:T(8,128)(2,1)S(1)}, bf16[32,2048]{1,0:T(8,128)(2,1)S(1)}, u32[]{:S(2)}, u32[]{:S(2)}) collective-permute-start(bf16[32,2048]{1,0:T(8,128)(2,1)S(1)} %shard_map.230.refs_0_), channel_id=1, source_target_pairs={{1,0},{2,1},{3,2},{0,3},{5,4},{6,5},{7,6},{4,7},{9,8},{10,9},{11,1... | collective-permute-start | bytes 393224 | tf_op jit(solution)/shard_map/ppermute | solution.py:43
  362.4 20.7 %collective-permute-start.48 = (bf16[128,2048]{1,0:T(8,128)(2,1)S(1)}, bf16[128,2048]{1,0:T(8,128)(2,1)S(1)}, u32[]{:S(2)}, u32[]{:S(2)}) collective-permute-start(bf16[128,2048]{1,0:T(8,128)(2,1)S(1)} %shard_map.233.rest_4_), channel_id=1, source_target_pairs={{0,4},{1,5},{2,6},{3,7},{4,0},{5,1},{6,2},{7,3},{8,12},{9,13},{10,... | collective-permute-start | bytes 1572872 | tf_op jit(solution)/shard_map/ppermute | solution.py:39
  365.4 13.9 %collective-permute-start.42 = (bf16[64,2048]{1,0:T(8,128)(2,1)S(1)}, bf16[64,2048]{1,0:T(8,128)(2,1)S(1)}, u32[]{:S(2)}, u32[]{:S(2)}) collective-permute-start(bf16[64,2048]{1,0:T(8,128)(2,1)S(1)} %shard_map.231.rest_0_), channel_id=1, source_target_pairs={{1,0},{2,1},{3,2},{0,3},{5,4},{6,5},{7,6},{4,7},{9,8},{10,9},{11,1... | collective-permute-start | bytes 786440 | tf_op jit(solution)/shard_map/ppermute | solution.py:43
  368.4 11.0 %collective-permute-start.43 = (bf16[64,2048]{1,0:T(8,128)(2,1)S(1)}, bf16[64,2048]{1,0:T(8,128)(2,1)S(1)}, u32[]{:S(2)}, u32[]{:S(2)}) collective-permute-start(bf16[64,2048]{1,0:T(8,128)(2,1)S(1)} %shard_map.231.rest_0_), channel_id=1, source_target_pairs={{2,0},{3,1},{0,2},{1,3},{6,4},{7,5},{4,6},{5,7},{10,8},{11,9},{8,1... | collective-permute-start | bytes 786440 | tf_op jit(solution)/shard_map/ppermute | solution.py:43
  369.1 14.0 %collective-permute-start.44 = (bf16[64,2048]{1,0:T(8,128)(2,1)S(1)}, bf16[64,2048]{1,0:T(8,128)(2,1)S(1)}, u32[]{:S(2)}, u32[]{:S(2)}) collective-permute-start(bf16[64,2048]{1,0:T(8,128)(2,1)S(1)} %shard_map.231.rest_0_), channel_id=1, source_target_pairs={{3,0},{0,1},{1,2},{2,3},{7,4},{4,5},{5,6},{6,7},{11,8},{8,9},{9,10... | collective-permute-start | bytes 786440 | tf_op jit(solution)/shard_map/ppermute | solution.py:43
  404.0 10.4 %collective-permute-start.49 = (bf16[1024,512]{1,0:T(8,128)(2,1)S(1)}, bf16[1024,512]{1,0:T(8,128)(2,1)S(1)}, u32[]{:S(2)}, u32[]{:S(2)}) collective-permute-start(bf16[1024,512]{1,0:T(8,128)(2,1)S(1)} %get-tuple-element.334), channel_id=1, source_target_pairs={{0,8},{8,0},{16,24},{24,16},{1,9},{9,1},{17,25},{25,17},{2,10},{10... | collective-permute-start | bytes 3145736 | tf_op jit(solution)/shard_map/ppermute | solution.py:23
  414.5 16.1 %collective-permute-start.54 = (bf16[1024,1280]{1,0:T(8,128)(2,1)}, bf16[1024,1280]{1,0:T(8,128)(2,1)}, u32[]{:S(2)}, u32[]{:S(2)}) collective-permute-start(bf16[1024,1280]{1,0:T(8,128)(2,1)} %shard_map.237), channel_id=1, source_target_pairs={{0,8},{8,0},{16,24},{24,16},{1,9},{9,1},{17,25},{25,17},{2,10},{10... | collective-permute-start | bytes 7864328 | tf_op jit(solution)/shard_map/ppermute | solution.py:23
  414.6 75.4 %reduce-scatter.13.cloned.1.call-start = ((), (), s32[]{:S(2)}) async-start(), calls=%async_computation.12 | async-start | bytes 3276800 | tf_op jit(solution)/shard_map/reduce_scatter | solution.py:896
  414.7 15.9 %collective-permute-start.55 = (bf16[128,2048]{1,0:T(8,128)(2,1)S(1)}, bf16[128,2048]{1,0:T(8,128)(2,1)S(1)}, u32[]{:S(2)}, u32[]{:S(2)}) collective-permute-start(bf16[128,2048]{1,0:T(8,128)(2,1)S(1)} %shard_map.240.rest_5_), channel_id=1, source_target_pairs={{0,4},{1,5},{2,6},{3,7},{4,0},{5,1},{6,2},{7,3},{8,12},{9,13},{10,... | collective-permute-start | bytes 1572872 | tf_op jit(solution)/shard_map/ppermute | solution.py:39
  431.5 14.4 %collective-permute-start.53 = (bf16[512,512]{1,0:T(8,128)(2,1)S(1)}, bf16[512,512]{1,0:T(8,128)(2,1)S(1)}, u32[]{:S(2)}, u32[]{:S(2)}) collective-permute-start(bf16[512,512]{1,0:T(8,128)(2,1)S(1)} %shard_map.238), channel_id=1, source_target_pairs={{0,16},{8,24},{16,0},{24,8},{1,17},{9,25},{17,1},{25,9},{2,18},{10... | collective-permute-start | bytes 1572872 | tf_op jit(solution)/shard_map/ppermute | solution.py:27
  445.9 116.1 %reduce-scatter.15.cloned.1.call-start = ((), (), s32[]{:S(2)}) async-start(), calls=%async_computation.13 | async-start | bytes 2621440 | tf_op jit(solution)/shard_map/reduce_scatter | solution.py:896
  446.7 125.2 %reduce-scatter.17.cloned.1.call-start = ((), (), s32[]{:S(2)}) async-start(), calls=%async_computation.14 | async-start | bytes 1966080 | tf_op jit(solution)/shard_map/reduce_scatter | solution.py:896
  446.9 19.6 %collective-permute-start.61 = (bf16[64,2048]{1,0:T(8,128)(2,1)S(1)}, bf16[64,2048]{1,0:T(8,128)(2,1)}, u32[]{:S(2)}, u32[]{:S(2)}) collective-permute-start(bf16[64,2048]{1,0:T(8,128)(2,1)S(1)} %shard_map.244.rest_1_), channel_id=1, source_target_pairs={{1,0},{2,1},{3,2},{0,3},{5,4},{6,5},{7,6},{4,7},{9,8},{10,9},{11,1... | collective-permute-start | bytes 786440 | tf_op jit(solution)/shard_map/ppermute | solution.py:43
  448.1 20.3 %collective-permute-start.62 = (bf16[64,2048]{1,0:T(8,128)(2,1)S(1)}, bf16[64,2048]{1,0:T(8,128)(2,1)S(1)}, u32[]{:S(2)}, u32[]{:S(2)}) collective-permute-start(bf16[64,2048]{1,0:T(8,128)(2,1)S(1)} %shard_map.244.rest_1_), channel_id=1, source_target_pairs={{3,0},{0,1},{1,2},{2,3},{7,4},{4,5},{5,6},{6,7},{11,8},{8,9},{9,10... | collective-permute-start | bytes 786440 | tf_op jit(solution)/shard_map/ppermute | solution.py:43
  449.2 20.6 %collective-permute-start.63 = (bf16[64,2048]{1,0:T(8,128)(2,1)S(1)}, bf16[64,2048]{1,0:T(8,128)(2,1)S(1)}, u32[]{:S(2)}, u32[]{:S(2)}) collective-permute-start(bf16[64,2048]{1,0:T(8,128)(2,1)S(1)} %shard_map.244.rest_1_), channel_id=1, source_target_pairs={{2,0},{3,1},{0,2},{1,3},{6,4},{7,5},{4,6},{5,7},{10,8},{11,9},{8,1... | collective-permute-start | bytes 786440 | tf_op jit(solution)/shard_map/ppermute | solution.py:43
  450.9 20.7 %collective-permute-start.64 = (bf16[128,1280]{1,0:T(8,128)(2,1)S(1)}, bf16[128,1280]{1,0:T(8,128)(2,1)S(1)}, u32[]{:S(2)}, u32[]{:S(2)}) collective-permute-start(bf16[128,1280]{1,0:T(8,128)(2,1)S(1)} %slice.52), channel_id=1, source_target_pairs={{0,16},{8,24},{16,0},{24,8},{1,17},{9,25},{17,1},{25,9},{2,18},{10... | collective-permute-start | bytes 983048 | tf_op jit(solution)/shard_map/ppermute | solution.py:27
  465.8 23.4 %collective-permute-start.60 = (bf16[128,2048]{1,0:T(8,128)(2,1)S(1)}, bf16[128,2048]{1,0:T(8,128)(2,1)S(1)}, u32[]{:S(2)}, u32[]{:S(2)}) collective-permute-start(bf16[128,2048]{1,0:T(8,128)(2,1)S(1)} %get-tuple-element.360), channel_id=1, source_target_pairs={{0,4},{1,5},{2,6},{3,7},{4,0},{5,1},{6,2},{7,3},{8,12},{9,13},{10,... | collective-permute-start | bytes 1572872 | tf_op jit(solution)/shard_map/ppermute | solution.py:39
  466.5 17.1 %collective-permute-start.65 = (bf16[128,1024]{1,0:T(8,128)(2,1)S(1)}, bf16[128,1024]{1,0:T(8,128)(2,1)S(1)}, u32[]{:S(2)}, u32[]{:S(2)}) collective-permute-start(bf16[128,1024]{1,0:T(8,128)(2,1)S(1)} %slice.53), channel_id=1, source_target_pairs={{0,16},{8,24},{16,0},{24,8},{1,17},{9,25},{17,1},{25,9},{2,18},{10... | collective-permute-start | bytes 786440 | tf_op jit(solution)/shard_map/ppermute | solution.py:27
  468.4 18.7 %collective-permute-start.57 = (bf16[64,2048]{1,0:T(8,128)(2,1)S(1)}, bf16[64,2048]{1,0:T(8,128)(2,1)S(1)}, u32[]{:S(2)}, u32[]{:S(2)}) collective-permute-start(bf16[64,2048]{1,0:T(8,128)(2,1)S(1)} %get-tuple-element.357), channel_id=1, source_target_pairs={{0,1},{1,2},{2,3},{3,0},{4,5},{5,6},{6,7},{7,4},{8,9},{9,10},{10,1... | collective-permute-start | bytes 786440 | tf_op jit(solution)/shard_map/ppermute | solution.py:47
  469.8 18.0 %collective-permute-start.58 = (bf16[64,2048]{1,0:T(8,128)(2,1)S(1)}, bf16[64,2048]{1,0:T(8,128)(2,1)S(1)}, u32[]{:S(2)}, u32[]{:S(2)}) collective-permute-start(bf16[64,2048]{1,0:T(8,128)(2,1)S(1)} %get-tuple-element.358), channel_id=1, source_target_pairs={{0,3},{1,0},{2,1},{3,2},{4,7},{5,4},{6,5},{7,6},{8,11},{9,8},{10,9... | collective-permute-start | bytes 786440 | tf_op jit(solution)/shard_map/ppermute | solution.py:47
  471.6 16.9 %collective-permute-start.59 = (bf16[64,2048]{1,0:T(8,128)(2,1)S(1)}, bf16[64,2048]{1,0:T(8,128)(2,1)S(1)}, u32[]{:S(2)}, u32[]{:S(2)}) collective-permute-start(bf16[64,2048]{1,0:T(8,128)(2,1)S(1)} %get-tuple-element.359), channel_id=1, source_target_pairs={{0,2},{1,3},{2,0},{3,1},{4,6},{5,7},{6,4},{7,5},{8,10},{9,11},{10,... | collective-permute-start | bytes 786440 | tf_op jit(solution)/shard_map/ppermute | solution.py:47
  490.0 21.2 %collective-permute-start.70 = (bf16[1024,768]{1,0:T(8,128)(2,1)S(1)}, bf16[1024,768]{1,0:T(8,128)(2,1)S(1)}, u32[]{:S(2)}, u32[]{:S(2)}) collective-permute-start(bf16[1024,768]{1,0:T(8,128)(2,1)S(1)} %shard_map.245), channel_id=1, source_target_pairs={{0,8},{8,0},{16,24},{24,16},{1,9},{9,1},{17,25},{25,17},{2,10},{10... | collective-permute-start | bytes 4718600 | tf_op jit(solution)/shard_map/ppermute | solution.py:23
  490.0 11.3 %collective-permute-start.71 = (f32[2,8,2048]{2,1,0:T(8,128)S(1)}, f32[2,8,2048]{2,1,0:T(8,128)S(1)}, u32[]{:S(2)}, u32[]{:S(2)}) collective-permute-start(f32[2,8,2048]{2,1,0:T(8,128)S(1)} %pad_maximum_fusion.1), channel_id=1, source_target_pairs={{0,16},{8,24},{16,0},{24,8},{1,17},{9,25},{17,1},{25,9},{2,18},{10... | collective-permute-start | bytes 393224 | tf_op jit(solution)/shard_map/ppermute | solution.py:27
  490.9 12.0 %collective-permute-start.72 = (f32[2,8,2048]{2,1,0:T(8,128)S(1)}, f32[2,8,2048]{2,1,0:T(8,128)S(1)}, u32[]{:S(2)}, u32[]{:S(2)}) collective-permute-start(f32[2,8,2048]{2,1,0:T(8,128)S(1)} %pad_maximum_fusion.1), channel_id=1, source_target_pairs={{0,8},{8,0},{16,24},{24,16},{1,9},{9,1},{17,25},{25,17},{2,10},{10... | collective-permute-start | bytes 393224 | tf_op jit(solution)/shard_map/ppermute | solution.py:23
  491.2 13.6 %collective-permute-start.73 = (f32[2,8,2048]{2,1,0:T(8,128)S(1)}, f32[2,8,2048]{2,1,0:T(8,128)S(1)}, u32[]{:S(2)}, u32[]{:S(2)}) collective-permute-start(f32[2,8,2048]{2,1,0:T(8,128)S(1)} %pad_maximum_fusion.1), channel_id=1, source_target_pairs={{0,24},{8,16},{16,8},{24,0},{1,25},{9,17},{17,9},{25,1},{2,26},{10... | collective-permute-start | bytes 393224 | tf_op jit(solution)/shard_map/ppermute | solution.py:35
  496.2 15.0 %collective-permute-start.66 = (bf16[64,2048]{1,0:T(8,128)(2,1)S(1)}, bf16[64,2048]{1,0:T(8,128)(2,1)S(1)}, u32[]{:S(2)}, u32[]{:S(2)}) collective-permute-start(bf16[64,2048]{1,0:T(8,128)(2,1)S(1)} %shard_map.247.refs_0_), channel_id=1, source_target_pairs={{0,4},{1,5},{2,6},{3,7},{4,0},{5,1},{6,2},{7,3},{8,12},{9,13},{10,... | collective-permute-start | bytes 786440 | tf_op jit(solution)/shard_map/ppermute | solution.py:39
  516.9 11.1 %collective-permute-start.81 = (bf16[128,1280]{1,0:T(8,128)(2,1)S(1)}, bf16[128,1280]{1,0:T(8,128)(2,1)S(1)}, u32[]{:S(2)}, u32[]{:S(2)}) collective-permute-start(bf16[128,1280]{1,0:T(8,128)(2,1)S(1)} %slice.55), channel_id=1, source_target_pairs={{0,16},{8,24},{16,0},{24,8},{1,17},{9,25},{17,1},{25,9},{2,18},{10... | collective-permute-start | bytes 983048 | tf_op jit(solution)/shard_map/ppermute | solution.py:27
  518.1 11.1 %collective-permute-start.74 = (bf16[32,2048]{1,0:T(8,128)(2,1)S(1)}, bf16[32,2048]{1,0:T(8,128)(2,1)S(1)}, u32[]{:S(2)}, u32[]{:S(2)}) collective-permute-start(bf16[32,2048]{1,0:T(8,128)(2,1)S(1)} %shard_map.248.refs_0_), channel_id=1, source_target_pairs={{1,0},{2,1},{3,2},{0,3},{5,4},{6,5},{7,6},{4,7},{9,8},{10,9},{11,1... | collective-permute-start | bytes 393224 | tf_op jit(solution)/shard_map/ppermute | solution.py:43
  520.8 11.5 %collective-permute-start.76 = (bf16[32,2048]{1,0:T(8,128)(2,1)S(1)}, bf16[32,2048]{1,0:T(8,128)(2,1)S(1)}, u32[]{:S(2)}, u32[]{:S(2)}) collective-permute-start(bf16[32,2048]{1,0:T(8,128)(2,1)S(1)} %shard_map.248.refs_0_), channel_id=1, source_target_pairs={{2,0},{3,1},{0,2},{1,3},{6,4},{7,5},{4,6},{5,7},{10,8},{11,9},{8,1... | collective-permute-start | bytes 393224 | tf_op jit(solution)/shard_map/ppermute | solution.py:43
  528.1 10.9 %collective-permute-start.78 = (f32[2,8,2048]{2,1,0:T(8,128)S(1)}, f32[2,8,2048]{2,1,0:T(8,128)S(1)}, u32[]{:S(2)}, u32[]{:S(2)}) collective-permute-start(f32[2,8,2048]{2,1,0:T(8,128)S(1)} %add_add_fusion.1), channel_id=1, source_target_pairs={{64,0},{96,32},{0,64},{32,96},{65,1},{97,33},{1,65},{33,97},{66,2}... | collective-permute-start | bytes 393224 | tf_op jit(solution)/shard_map/ppermute | solution.py:31
  529.3 11.0 %collective-permute-start.79 = (f32[2,8,2048]{2,1,0:T(8,128)S(1)}, f32[2,8,2048]{2,1,0:T(8,128)S(1)}, u32[]{:S(2)}, u32[]{:S(2)}) collective-permute-start(f32[2,8,2048]{2,1,0:T(8,128)S(1)} %add_add_fusion.1), channel_id=1, source_target_pairs={{96,0},{0,32},{32,64},{64,96},{97,1},{1,33},{33,65},{65,97},{98,2}... | collective-permute-start | bytes 393224 | tf_op jit(solution)/shard_map/ppermute | solution.py:31
  529.5 29.2 %collective-permute-start.83 = (bf16[64,2048]{1,0:T(8,128)(2,1)S(1)}, bf16[64,2048]{1,0:T(8,128)(2,1)S(1)}, u32[]{:S(2)}, u32[]{:S(2)}) collective-permute-start(bf16[64,2048]{1,0:T(8,128)(2,1)S(1)} %shard_map.249.rest_2_), channel_id=1, source_target_pairs={{1,0},{2,1},{3,2},{0,3},{5,4},{6,5},{7,6},{4,7},{9,8},{10,9},{11,1... | collective-permute-start | bytes 786440 | tf_op jit(solution)/shard_map/ppermute | solution.py:43
  532.3 26.4 %collective-permute-start.84 = (bf16[64,2048]{1,0:T(8,128)(2,1)S(1)}, bf16[64,2048]{1,0:T(8,128)(2,1)S(1)}, u32[]{:S(2)}, u32[]{:S(2)}) collective-permute-start(bf16[64,2048]{1,0:T(8,128)(2,1)S(1)} %shard_map.249.rest_2_), channel_id=1, source_target_pairs={{3,0},{0,1},{1,2},{2,3},{7,4},{4,5},{5,6},{6,7},{11,8},{8,9},{9,10... | collective-permute-start | bytes 786440 | tf_op jit(solution)/shard_map/ppermute | solution.py:43
  533.0 25.8 %collective-permute-start.85 = (bf16[64,2048]{1,0:T(8,128)(2,1)S(1)}, bf16[64,2048]{1,0:T(8,128)(2,1)S(1)}, u32[]{:S(2)}, u32[]{:S(2)}) collective-permute-start(bf16[64,2048]{1,0:T(8,128)(2,1)S(1)} %shard_map.249.rest_2_), channel_id=1, source_target_pairs={{2,0},{3,1},{0,2},{1,3},{6,4},{7,5},{4,6},{5,7},{10,8},{11,9},{8,1... | collective-permute-start | bytes 786440 | tf_op jit(solution)/shard_map/ppermute | solution.py:43
  540.3 18.4 %collective-permute-start.82 = (bf16[128,2048]{1,0:T(8,128)(2,1)S(1)}, bf16[128,2048]{1,0:T(8,128)(2,1)S(1)}, u32[]{:S(2)}, u32[]{:S(2)}) collective-permute-start(bf16[128,2048]{1,0:T(8,128)(2,1)S(1)} %shard_map.251.rest_6_), channel_id=1, source_target_pairs={{0,4},{1,5},{2,6},{3,7},{4,0},{5,1},{6,2},{7,3},{8,12},{9,13},{10,... | collective-permute-start | bytes 1572872 | tf_op jit(solution)/shard_map/ppermute | solution.py:39
  559.5 12.3 %collective-permute-start.91 = (f32[2,4,2048]{2,1,0:T(4,128)S(1)}, f32[2,4,2048]{2,1,0:T(4,128)S(1)}, u32[]{:S(2)}, u32[]{:S(2)}) collective-permute-start(f32[2,4,2048]{2,1,0:T(4,128)S(1)} %add_add_fusion.2), channel_id=1, source_target_pairs={{0,4},{1,5},{2,6},{3,7},{4,0},{5,1},{6,2},{7,3},{8,12},{9,13},{10,... | collective-permute-start | bytes 196616 | tf_op jit(solution)/shard_map/ppermute | solution.py:39
  563.0 12.0 %collective-permute-start.89 = (bf16[128,1024]{1,0:T(8,128)(2,1)S(1)}, bf16[128,1024]{1,0:T(8,128)(2,1)S(1)}, u32[]{:S(2)}, u32[]{:S(2)}) collective-permute-start(bf16[128,1024]{1,0:T(8,128)(2,1)S(1)} %slice.69), channel_id=1, source_target_pairs={{0,16},{8,24},{16,0},{24,8},{1,17},{9,25},{17,1},{25,9},{2,18},{10... | collective-permute-start | bytes 786440 | tf_op jit(solution)/shard_map/ppermute | solution.py:27
  (169 other events, 1614.3 us)
Sparse Core Ops, SparseCore 0:
  10.2 74.2 all-gather.3
  110.8 64.8 all-gather.7
  177.9 46.7 all-gather.5
  296.8 33.7 reduce-scatter.6
  332.9 29.3 reduce-scatter.8
  414.7 22.1 reduce-scatter.10
  446.0 31.1 reduce-scatter.12
  479.8 29.4 reduce-scatter.14
  516.0 27.7 reduce-scatter.16
where the time goes:
time: 601 us; the launch traced here: 590 us
  waiting for transfers between devices  204 us (34%)
  Pallas kernels  192 us (32%)
  starting transfers between devices  122 us (20%)
  local copies, waits for them, and re-layouts  53.4 us (9%)
  between operations  15.8 us (3%)
    pallas_call x52, Pallas kernels, call(): pl.pallas_call(body, grid_spec=pltpu.PrefetchScalarGridSpec(num_scalar_pr...  192 us
    all_gather x3, waiting for transfers between devices, gather_weights(): return lax.all_gather(shard, ('fsdp', 'ctx'), axis=1, tiled=True)  67.8 us
    unnamed x273, local copies, waits for them, and re-layouts  49.8 us
    ppermute x27, starting transfers between devices, from_z(): lax.ppermute(value, 'tp', [((i & 4) + (i + k) % 4, i) for i in range(8)])  38.7 us
    ppermute x24, starting transfers between devices, to_z(): lax.ppermute(value, 'tp', [(i, (i & 4) + (i + k) % 4) for i in range(8)])  37.3 us
    ppermute x27, waiting for transfers between devices, from_z(): lax.ppermute(value, 'tp', [((i & 4) + (i + k) % 4, i) for i in range(8)])  35.3 us
    ppermute x24, waiting for transfers between devices, to_z(): lax.ppermute(value, 'tp', [(i, (i & 4) + (i + k) % 4) for i in range(8)])  33.3 us
    ppermute x11, waiting for transfers between devices, swap_y(): return lax.ppermute(value, 'ctx', [(i, i ^ 2) for i in range(4)])  31.8 us
  transfers between devices with their start and end apart: 101, of which 42 were waited for; matrix products, arithmetic and copies ran while one was open for 1% of the time, Pallas kernels for 25%

commit v1 on v0

--- a/solution.py
+++ b/solution.py
@@ -1032,6 +1032,8 @@
         else:
             after = kept[l + 1]
             g, gm, gh, part = next_back_out(g, after[2], after[3], sums, w_out, slope)
+            out_after, up_after, qkv_after = scattered[l + 1]
+            up_half, gm = together(swap_half(up_after), gm)
         dq, own, to_y, send = attend_back(q, kvs, gm, qpos, kpos)
         from_core = swap_core(send)
         out_far = weight_grad(g, pinned(mixed, active), far)
@@ -1047,25 +1049,20 @@
         from_y = swap_y(add_late(to_y, from_core))
         out_got = swap_core(out_far)
         up_far = weight_grad(nm, pinned(gh), far)
-        if last:
-            out_got, up_far = together(out_got, up_far)
-        else:
-            out_got, up_far, late_far = together(out_got, up_far, late_far)
+        out_got, up_far = together(out_got, up_far)
         out_near = weight_grad(g, pinned(mixed, active), near, out_got)
         up_got, out_near = together(swap_core(up_far), out_near)
         up_near = weight_grad(nm, pinned(gh), near, up_got)
         if last:
             from_y, out_near, up_near = together(from_y, out_near, up_near)
         else:
-            out_after, up_after, qkv_after = scattered[l + 1]
             from_y, out_near, up_near, qkv_after = together(from_y, out_near, up_near, qkv_after)
-            out_half, up_half = swap_half(out_after), swap_half(up_after)
         out_sum = scatter_weight_grad(out_near)
         gp, terms, small[l] = back_in(
             dq, own, from_core, from_y, tables, gh, w_in, x, stats, vec, l, part
         )
         if not last:
-            late_firsts, out_half, up_half, gp = together(late_firsts, out_half, up_half, gp)
+            late_firsts, late_far, gp = together(late_firsts, late_far, gp)
         held, moving = tp_1(terms)
         up_sum = scatter_weight_grad(up_near)
         qkv_far = weight_grad(na, (gp,), far)
@@ -1085,7 +1082,8 @@
         qkv_near = weight_grad(na, (gp,), near, qkv_got)
         qkv_sum = scatter_weight_grad(qkv_near)
         if last:
-            seconds, qkv_near, up_sum = together(seconds, qkv_near, up_sum)
+            out_half = swap_half(out_sum)
+            seconds, qkv_near, up_sum, out_half = together(seconds, qkv_near, up_sum, out_half)
             sums = tp_pieces(first, firsts, *tp_4(second, seconds))
         else:
             total = pair_up(total, parts)
@@ -1102,8 +1100,11 @@
             parts = around(wide, from_z)
             late_pieces = tp_pieces(late_first, late_firsts, late_near, late_far)
             activations = last_stream(tokens, row_at, kept[-1][2], late_pieces, vec, LAYERS - 1)
-            sum_far, firsts, parts, activations = together(sum_far, firsts, parts, activations)
-            halves[0] += [swap_half(up_sum), swap_half(qkv_sum)]
+            last_halves = [swap_half(up_sum), swap_half(qkv_sum)]
+            sum_far, firsts, parts, activations, last_halves = together(
+                sum_far, firsts, parts, activations, last_halves
+            )
+            halves[0] += last_halves
             wide = pair_up(wide, parts)
             wide = wide + swap_tp(wide, 4)
             sums = tp_pieces(first, firsts, sum_near, sum_far)

time: 601 us -> 586 us (0.975)
  waiting for transfers between devices: 204 us -> 182 us
    ppermute x11, waiting for transfers between devices: 31.8 us -> 15.9 us  [swap_y(): return lax.ppermute(value, 'ctx', [(i, i ^ 2) for i in range(4)])]
    ppermute x13, waiting for transfers between devices: 20.1 us -> 10.6 us  [swap_tp(): return lax.ppermute(value, 'tp', [(i, i ^ k) for i in range(8)])]
    unnamed x273 -> x287, local copies, waits for them, and re-layouts: 49.8 us -> 52.1 us
  transfers between devices with their start and end apart: 101 -> 101, of which waited for: 42 -> 41; matrix products, arithmetic and copies ran while one was open for 1% -> 2% of each run, Pallas kernels for 25% -> 29%
where the time goes in v1:
time: 586 us; the launch traced here: 575 us
  Pallas kernels  192 us (33%)
  waiting for transfers between devices  182 us (31%)
  starting transfers between devices  125 us (21%)
  local copies, waits for them, and re-layouts  57.4 us (10%)
  between operations  15.8 us (3%)
    pallas_call x52, Pallas kernels, call(): pl.pallas_call(body, grid_spec=pltpu.PrefetchScalarGridSpec(num_scalar_pr...  192 us
    all_gather x3, waiting for transfers between devices, gather_weights(): return lax.all_gather(shard, ('fsdp', 'ctx'), axis=1, tiled=True)  67.8 us
    unnamed x287, local copies, waits for them, and re-layouts  52.1 us
    ppermute x27, starting transfers between devices, from_z(): lax.ppermute(value, 'tp', [((i & 4) + (i + k) % 4, i) for i in range(8)])  39.5 us
    ppermute x24, starting transfers between devices, to_z(): lax.ppermute(value, 'tp', [(i, (i & 4) + (i + k) % 4) for i in range(8)])  36.9 us
    ppermute x24, waiting for transfers between devices, to_z(): lax.ppermute(value, 'tp', [(i, (i & 4) + (i + k) % 4) for i in range(8)])  36.3 us
    ppermute x27, waiting for transfers between devices, from_z(): lax.ppermute(value, 'tp', [((i & 4) + (i + k) % 4, i) for i in range(8)])  35.2 us
    ppermute x13, starting transfers between devices, swap_tp(): return lax.ppermute(value, 'tp', [(i, i ^ k) for i in range(8)])  30.6 us
  transfers between devices with their start and end apart: 101, of which 41 were waited for; matrix products, arithmetic and copies ran while one was open for 2% of the time, Pallas kernels for 29%

profile of v1, /device:TPU:0, one launch (start us, length us, event | category | flops | bytes accessed | tf_op | source)
XLA Modules:
  0.0 575.2 jit_solution(2173408249370029934)
XLA Ops:
  16.8 67.7 %all-gather.4.cloned.1.call-done.w_ref.rest_6_ = bf16[12,2048,256]{2,1,0:T(8,128)(2,1)} async-done(((bf16[12,128,256]{2,1,0:T(8,128)(2,1)}), bf16[12,2048,256]{2,1,0:T(8,128)(2,1)}) %all-gather.4.cloned.1.call-update) | async-done | bytes 12582928 | tf_op jit(solution)/shard_map/all_gather | solution.py:51
  84.6 9.2 %shard_map.206 = (bf16[512,2048]{1,0:T(8,128)(2,1)S(1)}, f32[512,128]{1,0:T(8,128)S(1)}, bf16[512,2048]{1,0:T(8,128)(2,1)S(1)}, bf16[512,2048]{1,0:T(8,128)(2,1)...) custom-call(s32[16]{0:T(128)S(1)} %pad_add_fusion.1.row_ref, bf16[2,256,2048]{2,1,0:T(8,128)(2,1)} %tok_ref.1, ...), custom_call_target="tpu_custom_call" | custom-call | flops 1610612736 | bytes 14552128 | tf_op jit(solution)/shard_map/pallas_call | solution.py:108
  98.0 7.6 %shard_map.207 = (bf16[512,1024]{1,0:T(8,128)(2,1)S(1)}, bf16[512,1024]{1,0:T(8,128)(2,1)S(1)}) custom-call(bf16[512,2048]{1,0:T(8,128)(2,1)S(1)} %get-tuple-element.227.n_ref.x_ref, bf16[12,2048,256]{2,1,0:T(8,128)(2,1)} %all-gather.4.cloned.1.call-done.w_ref.rest_6_, f32[1,1024]{1,0:T(1,128)S(1)} %get-tuple-element.446.b_ref), custom_call_target="tpu_custom_call" | custom-call | flops 2147483648 | bytes 8392704 | tf_op jit(solution)/shard_map/pallas_call | solution.py:108
  107.6 3.0 collective-permute-done.1.k2
  114.9 6.6 %shard_map.208 = (bf16[512,256]{1,0:T(8,128)(2,1)S(1)}, bf16[64,2048]{1,0:T(8,128)(2,1)S(1)}, bf16[64,2048]{1,0:T(8,128)(2,1)S(1)}, bf16[64,2048]{1,0:T(8,128)(2...) custom-call(bf16[512,256]{1,0:T(8,128)(2,1)S(1)} %get-tuple-element.225.q_ref, ...), custom_call_target="tpu_custom_call" | custom-call | flops 3221225472 | bytes 9971712 | tf_op jit(solution)/shard_map/pallas_call | solution.py:108
  122.2 2.9 collective-permute-start.6
  130.5 4.1 collective-permute-done.3.refs_1_
  134.6 5.0 collective-permute-done.4.refs_2_
  141.4 8.0 %collective-permute-done.6.b_ref = bf16[128,2048]{1,0:T(8,128)(2,1)S(1)} collective-permute-done((bf16[128,2048]{1,0:T(8,128)(2,1)S(1)}, bf16[128,2048]{1,0:T(8,128)(2,1)S(1)}, u32[]{:S(2)}, u32[]{:S(2)}) %collective-permute-start.6) | collective-permute-done | bytes 524320 | tf_op jit(solution)/shard_map/ppermute | solution.py:39
  149.6 2.9 collective-permute-start.7
  165.5 3.0 collective-permute-start.11
  172.5 3.7 collective-permute-done.12.refs_3_
  176.2 3.0 collective-permute-start.17
  182.1 7.1 %collective-permute-done.14.rest_1_ = bf16[64,2048]{1,0:T(8,128)(2,1)S(1)} collective-permute-done((bf16[64,2048]{1,0:T(8,128)(2,1)S(1)}, bf16[64,2048]{1,0:T(8,128)(2,1)S(1)}, u32[]{:S(2)}, u32[]{:S(2)}) %collective-permute-start.14) | collective-permute-done | bytes 262176 | tf_op jit(solution)/shard_map/ppermute | solution.py:43
  190.2 2.7 collective-permute-done.16.rest_3_
  193.7 9.2 %shard_map.214 = (bf16[512,2048]{1,0:T(8,128)(2,1)S(1)}, f32[512,128]{1,0:T(8,128)S(1)}, bf16[512,2048]{1,0:T(8,128)(2,1)S(1)}, bf16[512,2048]{1,0:T(8,128)(2,1)...) custom-call(bf16[512,2048]{1,0:T(8,128)(2,1)} %copy-done.3, bf16[64,2048]{1,0:T(8,128)(2,1)} %copy-done.34, ...), custom_call_target="tpu_custom_call" | custom-call | flops 1610612736 | bytes 16649216 | tf_op jit(solution)/shard_map/pallas_call | solution.py:108
  207.4 7.7 %shard_map.215 = (bf16[512,1024]{1,0:T(8,128)(2,1)S(1)}, bf16[512,1024]{1,0:T(8,128)(2,1)S(1)}) custom-call(bf16[512,2048]{1,0:T(8,128)(2,1)S(1)} %get-tuple-element.261.n_ref.x_ref, bf16[7,2048,256]{2,1,0:T(8,128)(2,1)} %all-gather.6.cloned.1.call-done.rest_7_.w_ref, f32[1,1024]{1,0:T(1,128)S(1)} %get-tuple-element.445.b_ref), custom_call_target="tpu_custom_call" | custom-call | flops 2147483648 | bytes 8392704 | tf_op jit(solution)/shard_map/pallas_call | solution.py:108
  217.0 9.2 %collective-permute-done.19.k2 = bf16[512,512]{1,0:T(8,128)(2,1)S(1)} collective-permute-done((bf16[512,512]{1,0:T(8,128)(2,1)S(1)}, bf16[512,512]{1,0:T(8,128)(2,1)S(1)}, u32[]{:S(2)}, u32[]{:S(2)}) %collective-permute-start.19) | collective-permute-done | bytes 524320 | tf_op jit(solution)/shard_map/ppermute | solution.py:27
  229.5 7.6 %shard_map.216 = (bf16[512,256]{1,0:T(8,128)(2,1)S(1)}, bf16[64,2048]{1,0:T(8,128)(2,1)S(1)}, bf16[64,2048]{1,0:T(8,128)(2,1)S(1)}, bf16[64,2048]{1,0:T(8,128)(2...) custom-call(bf16[512,256]{1,0:T(8,128)(2,1)S(1)} %copy-done.102, ...), custom_call_target="tpu_custom_call" | custom-call | flops 3221225472 | bytes 9971712 | tf_op jit(solution)/shard_map/pallas_call | solution.py:108
  237.1 2.8 collective-permute-start.24
  245.2 10.5 %shard_map.217 = (bf16[512,2048]{1,0:T(8,128)(2,1)S(1)}, bf16[512,256]{1,0:T(8,128)(2,1)S(1)}, bf16[512,1024]{1,0:T(8,128)(2,1)S(1)}, f32[8,2048]{1,0:T(8,128)S(1)}) custom-call(s32[16]{0:T(128)S(1)} %pad_add_fusion.1.row_ref, bf16[2,256,2048]{2,1,0:T(8,128)(2,1)} %cot_ref.1, bf16[5,2048,256]{2,1,0:T(8,128)(2,1)} %all-gather.8.cloned.1.call-done.w_ref, ...), custom_call_target="tpu_custom_call" | custom-call | flops 2684354560 | bytes 10813504 | tf_op jit(solution)/shard_map/pallas_call | solution.py:108
  258.1 4.0 shard_map.218
  265.1 2.6 collective-permute-start.28
  268.0 5.2 shard_map.221
  276.0 5.9 %shard_map.223 = bf16[1024,1024]{1,0:T(8,128)(2,1)} custom-call(s32[8]{0:T(128)S(1)} %get-tuple-element.286.block_ref, bf16[512,2048]{1,0:T(8,128)(2,1)} %copy-done.5, bf16[512,1024]{1,0:T(8,128)(2,1)} %copy-done.6), custom_call_target="tpu_custom_call" | custom-call | flops 1073741824 | bytes 5242912 | tf_op jit(solution)/shard_map/pallas_call | solution.py:108
  283.6 6.3 %shard_map.224 = bf16[1024,1280]{1,0:T(8,128)(2,1)} custom-call(s32[8]{0:T(128)S(1)} %get-tuple-element.295.block_ref, bf16[512,2048]{1,0:T(8,128)(2,1)} %copy-done, bf16[512,256]{1,0:T(8,128)(2,1)} %copy-done.33, bf16[512,1024]{1,0:T(8,128)(2,1)} %copy-done.14, bf16[1024,1280]{1,0:T(8,128)(2,1)S(1)} %collective-permute-done.31.rest_2_), custom_call_target="tpu_custom_call" | custom-call | flops 1342177280 | bytes 8650784 | tf_op jit(solution)/shard_map/pallas_call | solution.py:108
  290.0 6.7 %shard_map.225 = bf16[1024,1024]{1,0:T(8,128)(2,1)} custom-call(s32[8]{0:T(128)S(1)} %get-tuple-element.295.block_ref, bf16[512,2048]{1,0:T(8,128)(2,1)} %copy-done.5, bf16[512,1024]{1,0:T(8,128)(2,1)} %copy-done.6, bf16[1024,1024]{1,0:T(8,128)(2,1)} %collective-permute-done.32.rest_1_), custom_call_target="tpu_custom_call" | custom-call | flops 1073741824 | bytes 7340064 | tf_op jit(solution)/shard_map/pallas_call | solution.py:108
  297.5 12.6 %shard_map.226 = (bf16[512,768]{1,0:T(8,128)(2,1)S(1)}, bf16[64,2048]{1,0:T(8,128)(2,1)S(1)}, bf16[64,2048]{1,0:T(8,128)(2,1)S(1)}, bf16[64,2048]{1,0:T(8,128)(2...) custom-call(f32[512,256]{1,0:T(8,128)} %copy-done.40, ...), custom_call_target="tpu_custom_call" | custom-call | flops 3758096384 | bytes 14680064 | tf_op jit(solution)/shard_map/pallas_call | solution.py:108
  311.5 2.6 collective-permute-start.36
  314.6 2.8 collective-permute-start.34
  319.2 3.4 shard_map.227
  324.2 3.8 collective-permute-done.34.refs_2_
  338.7 2.8 collective-permute-start.37
  351.1 2.7 collective-permute-start.42
  355.4 4.4 shard_map.232
  362.4 3.1 collective-permute-start.50
  365.5 2.9 collective-permute-start.47
  372.1 7.3 %collective-permute-done.47.rest_1_ = bf16[64,2048]{1,0:T(8,128)(2,1)S(1)} collective-permute-done((bf16[64,2048]{1,0:T(8,128)(2,1)S(1)}, bf16[64,2048]{1,0:T(8,128)(2,1)S(1)}, u32[]{:S(2)}, u32[]{:S(2)}) %collective-permute-start.47) | collective-permute-done | bytes 262176 | tf_op jit(solution)/shard_map/ppermute | solution.py:43
  379.4 3.7 collective-permute-done.49.rest_3_
  384.0 12.2 %shard_map.234 = (bf16[512,2048]{1,0:T(8,128)(2,1)S(1)}, bf16[512,256]{1,0:T(8,128)(2,1)S(1)}, bf16[512,1024]{1,0:T(8,128)(2,1)S(1)}, f32[8,2048]{1,0:T(8,128)S(1)}) custom-call(bf16[512,2048]{1,0:T(8,128)(2,1)} %copy-done, bf16[512,2048]{1,0:T(8,128)(2,1)} %copy-done.1, f32[512,128]{1,0:T(8,128)S(1)} %get-tuple-element.301.stat_ref, ...), custom_call_target="tpu_custom_call" | custom-call | flops 2684354560 | bytes 15269888 | tf_op jit(solution)/shard_map/pallas_call | solution.py:108
  399.8 4.0 shard_map.235
  407.7 6.3 %shard_map.237 = bf16[1024,1280]{1,0:T(8,128)(2,1)} custom-call(s32[8]{0:T(128)S(1)} %get-tuple-element.286.block_ref, bf16[512,2048]{1,0:T(8,128)(2,1)} %copy-done.2, bf16[512,256]{1,0:T(8,128)(2,1)} %copy-done.28, bf16[512,1024]{1,0:T(8,128)(2,1)} %copy-done.7), custom_call_target="tpu_custom_call" | custom-call | flops 1342177280 | bytes 6029344 | tf_op jit(solution)/shard_map/pallas_call | solution.py:108
  416.6 5.8 %shard_map.239 = bf16[1024,1024]{1,0:T(8,128)(2,1)} custom-call(s32[8]{0:T(128)S(1)} %get-tuple-element.286.block_ref, bf16[512,2048]{1,0:T(8,128)(2,1)} %copy-done.4, bf16[512,1024]{1,0:T(8,128)(2,1)} %copy-done.9), custom_call_target="tpu_custom_call" | custom-call | flops 1073741824 | bytes 5242912 | tf_op jit(solution)/shard_map/pallas_call | solution.py:108
  423.8 7.0 %shard_map.240 = bf16[1024,1280]{1,0:T(8,128)(2,1)} custom-call(s32[8]{0:T(128)S(1)} %get-tuple-element.295.block_ref, bf16[512,2048]{1,0:T(8,128)(2,1)} %copy-done.2, bf16[512,256]{1,0:T(8,128)(2,1)} %copy-done.28, bf16[512,1024]{1,0:T(8,128)(2,1)} %copy-done.7, bf16[1024,1280]{1,0:T(8,128)(2,1)} %collective-permute-done.56.rest_2_), custom_call_target="tpu_custom_call" | custom-call | flops 1342177280 | bytes 8650784 | tf_op jit(solution)/shard_map/pallas_call | solution.py:108
  430.9 6.6 %shard_map.241 = bf16[1024,1024]{1,0:T(8,128)(2,1)} custom-call(s32[8]{0:T(128)S(1)} %get-tuple-element.295.block_ref, bf16[512,2048]{1,0:T(8,128)(2,1)} %copy-done.4, bf16[512,1024]{1,0:T(8,128)(2,1)} %copy-done.9, bf16[1024,1024]{1,0:T(8,128)(2,1)} %collective-permute-done.57.rest_1_), custom_call_target="tpu_custom_call" | custom-call | flops 1073741824 | bytes 7340064 | tf_op jit(solution)/shard_map/pallas_call | solution.py:108
  440.5 3.0 collective-permute-start.62
  445.9 3.1 collective-permute-start.65
  449.1 12.7 %shard_map.242 = (bf16[512,768]{1,0:T(8,128)(2,1)S(1)}, bf16[64,2048]{1,0:T(8,128)(2,1)S(1)}, bf16[64,2048]{1,0:T(8,128)(2,1)S(1)}, bf16[64,2048]{1,0:T(8,128)(2...) custom-call(f32[512,256]{1,0:T(8,128)} %copy-done.39, ...), custom_call_target="tpu_custom_call" | custom-call | flops 3758096384 | bytes 14680064 | tf_op jit(solution)/shard_map/pallas_call | solution.py:108
  469.0 3.3 shard_map.245
  472.4 3.7 collective-permute-done.58.refs_1_
  485.1 3.2 collective-permute-start.66
  490.7 3.2 collective-permute-start.68
  493.9 3.3 collective-permute-done.67.refs_1_
  500.6 4.4 shard_map.250
  507.3 2.6 collective-permute-start.74
  514.5 2.7 collective-permute-done.81.refs_3_
  523.8 4.2 collective-permute-done.79
  528.1 4.2 collective-permute-start.86
  535.5 2.6 collective-permute-start.85
  541.1 5.9 %collective-permute-done.88 = f32[2,4,2048]{2,1,0:T(4,128)S(1)} collective-permute-done((f32[2,4,2048]{2,1,0:T(4,128)S(1)}, f32[2,4,2048]{2,1,0:T(4,128)S(1)}, u32[]{:S(2)}, u32[]{:S(2)}) %collective-permute-start.88) | collective-permute-done | bytes 65568 | tf_op jit(solution)/shard_map/ppermute | solution.py:43
  547.5 4.7 shard_map.252
  552.7 2.8 collective-permute-start.91
  557.4 6.3 %shard_map.253 = f32[2,256,2048]{2,1,0:T(8,128)} custom-call(s32[16]{0:T(128)S(1)} %copy-done.96, bf16[512,2048]{1,0:T(8,128)(2,1)} %copy-done.2, bf16[512,2048]{1,0:T(8,128)(2,1)} %copy-done.3, bf16[64,2048]{1,0:T(8,128)(2,1)} %copy-done.32, bf16[64,2048]{1,0:T(8,128)(2,1)} %copy-done.120, bf16[64,2048]{1,0:T(8,128)(2,1)} %copy-done.122, ...), custom_call_target="tpu_custom_call" | custom-call | bytes 10747968 | tf_op jit(solution)/shard_map/pallas_call | solution.py:108
  563.7 4.1 shard_map.254
  (538 shorter events, 171.2 us)
Async XLA Ops:
  7.2 77.4 %all-gather.4.cloned.1.call-start = ((), (), s32[]{:S(2)}) async-start(), calls=%async_computation.6 | async-start | bytes 13369344 | tf_op jit(solution)/shard_map/all_gather | solution.py:51
  9.4 183.5 %all-gather.6.cloned.1.call-start = ((), (), s32[]{:S(2)}) async-start(), calls=%async_computation.7 | async-start | bytes 7798784 | tf_op jit(solution)/shard_map/all_gather | solution.py:51
  96.5 14.2 %collective-permute-start.1 = (bf16[512,512]{1,0:T(8,128)(2,1)S(1)}, bf16[512,512]{1,0:T(8,128)(2,1)S(1)}, u32[]{:S(2)}, u32[]{:S(2)}) collective-permute-start(bf16[512,512]{1,0:T(8,128)(2,1)S(1)} %get-tuple-element.226.k0), channel_id=1, source_target_pairs={{0,16},{8,24},{16,0},{24,8},{1,17},{9,25},{17,1},{25,9},{2,18},{10... | collective-permute-start | bytes 1572872 | tf_op jit(solution)/shard_map/ppermute | solution.py:27
  110.7 115.5 %all-gather.8.cloned.1.call-start = ((), (), s32[]{:S(2)}) async-start(), calls=%async_computation.8 | async-start | bytes 5570560 | tf_op jit(solution)/shard_map/all_gather | solution.py:51
  122.2 27.2 %collective-permute-start.6 = (bf16[128,2048]{1,0:T(8,128)(2,1)S(1)}, bf16[128,2048]{1,0:T(8,128)(2,1)S(1)}, u32[]{:S(2)}, u32[]{:S(2)}) collective-permute-start(bf16[128,2048]{1,0:T(8,128)(2,1)S(1)} %get-tuple-element.238), channel_id=1, source_target_pairs={{0,4},{1,5},{2,6},{3,7},{4,0},{5,1},{6,2},{7,3},{8,12},{9,13},{10,... | collective-permute-start | bytes 1572872 | tf_op jit(solution)/shard_map/ppermute | solution.py:39
  126.8 12.8 %collective-permute-start.4 = (bf16[64,2048]{1,0:T(8,128)(2,1)S(1)}, bf16[64,2048]{1,0:T(8,128)(2,1)S(1)}, u32[]{:S(2)}, u32[]{:S(2)}) collective-permute-start(bf16[64,2048]{1,0:T(8,128)(2,1)S(1)} %get-tuple-element.236), channel_id=1, source_target_pairs={{0,3},{1,0},{2,1},{3,2},{4,7},{5,4},{6,5},{7,6},{8,11},{9,8},{10,9... | collective-permute-start | bytes 786440 | tf_op jit(solution)/shard_map/ppermute | solution.py:47
  128.5 12.9 %collective-permute-start.5 = (bf16[64,2048]{1,0:T(8,128)(2,1)S(1)}, bf16[64,2048]{1,0:T(8,128)(2,1)S(1)}, u32[]{:S(2)}, u32[]{:S(2)}) collective-permute-start(bf16[64,2048]{1,0:T(8,128)(2,1)S(1)} %get-tuple-element.237), channel_id=1, source_target_pairs={{0,2},{1,3},{2,0},{3,1},{4,6},{5,7},{6,4},{7,5},{8,10},{9,11},{10,... | collective-permute-start | bytes 786440 | tf_op jit(solution)/shard_map/ppermute | solution.py:47
  149.6 15.8 %collective-permute-start.7 = (bf16[64,2048]{1,0:T(8,128)(2,1)S(1)}, bf16[64,2048]{1,0:T(8,128)(2,1)S(1)}, u32[]{:S(2)}, u32[]{:S(2)}) collective-permute-start(bf16[64,2048]{1,0:T(8,128)(2,1)S(1)} %shard_map.210.refs_0_), channel_id=1, source_target_pairs={{0,4},{1,5},{2,6},{3,7},{4,0},{5,1},{6,2},{7,3},{8,12},{9,13},{10,... | collective-permute-start | bytes 786440 | tf_op jit(solution)/shard_map/ppermute | solution.py:39
  165.4 166.0 %reduce-scatter.7.cloned.1.call-start = ((), (), s32[]{:S(2)}) async-start(), calls=%async_computation.9 | async-start | bytes 3276800 | tf_op jit(solution)/shard_map/reduce_scatter | solution.py:896
  176.2 16.7 %collective-permute-start.17 = (bf16[128,2048]{1,0:T(8,128)(2,1)S(1)}, bf16[128,2048]{1,0:T(8,128)(2,1)S(1)}, u32[]{:S(2)}, u32[]{:S(2)}) collective-permute-start(bf16[128,2048]{1,0:T(8,128)(2,1)S(1)} %shard_map.213.rest_4_), channel_id=1, source_target_pairs={{0,4},{1,5},{2,6},{3,7},{4,0},{5,1},{6,2},{7,3},{8,12},{9,13},{10,... | collective-permute-start | bytes 1572872 | tf_op jit(solution)/shard_map/ppermute | solution.py:39
  179.1 10.1 %collective-permute-start.14 = (bf16[64,2048]{1,0:T(8,128)(2,1)S(1)}, bf16[64,2048]{1,0:T(8,128)(2,1)S(1)}, u32[]{:S(2)}, u32[]{:S(2)}) collective-permute-start(bf16[64,2048]{1,0:T(8,128)(2,1)S(1)} %shard_map.212.rest_0_), channel_id=1, source_target_pairs={{1,0},{2,1},{3,2},{0,3},{5,4},{6,5},{7,6},{4,7},{9,8},{10,9},{11,1... | collective-permute-start | bytes 786440 | tf_op jit(solution)/shard_map/ppermute | solution.py:43
  181.2 11.6 %collective-permute-start.16 = (bf16[64,2048]{1,0:T(8,128)(2,1)S(1)}, bf16[64,2048]{1,0:T(8,128)(2,1)S(1)}, u32[]{:S(2)}, u32[]{:S(2)}) collective-permute-start(bf16[64,2048]{1,0:T(8,128)(2,1)S(1)} %shard_map.212.rest_0_), channel_id=1, source_target_pairs={{3,0},{0,1},{1,2},{2,3},{7,4},{4,5},{5,6},{6,7},{11,8},{8,9},{9,10... | collective-permute-start | bytes 786440 | tf_op jit(solution)/shard_map/ppermute | solution.py:43
  206.3 19.9 %collective-permute-start.19 = (bf16[512,512]{1,0:T(8,128)(2,1)S(1)}, bf16[512,512]{1,0:T(8,128)(2,1)S(1)}, u32[]{:S(2)}, u32[]{:S(2)}) collective-permute-start(bf16[512,512]{1,0:T(8,128)(2,1)S(1)} %get-tuple-element.260.k0), channel_id=1, source_target_pairs={{0,16},{8,24},{16,0},{24,8},{1,17},{9,25},{17,1},{25,9},{2,18},{10... | collective-permute-start | bytes 1572872 | tf_op jit(solution)/shard_map/ppermute | solution.py:27
  207.0 19.2 %collective-permute-start.18 = (bf16[512,512]{1,0:T(8,128)(2,1)S(1)}, bf16[512,512]{1,0:T(8,128)(2,1)S(1)}, u32[]{:S(2)}, u32[]{:S(2)}) collective-permute-start(bf16[512,512]{1,0:T(8,128)(2,1)S(1)} %get-tuple-element.260.k0), channel_id=1, source_target_pairs={{0,8},{8,0},{16,24},{24,16},{1,9},{9,1},{17,25},{25,17},{2,10},{10... | collective-permute-start | bytes 1572872 | tf_op jit(solution)/shard_map/ppermute | solution.py:23
  237.1 21.0 %collective-permute-start.24 = (bf16[128,2048]{1,0:T(8,128)(2,1)S(1)}, bf16[128,2048]{1,0:T(8,128)(2,1)S(1)}, u32[]{:S(2)}, u32[]{:S(2)}) collective-permute-start(bf16[128,2048]{1,0:T(8,128)(2,1)S(1)} %get-tuple-element.269), channel_id=1, source_target_pairs={{0,4},{1,5},{2,6},{3,7},{4,0},{5,1},{6,2},{7,3},{8,12},{9,13},{10,... | collective-permute-start | bytes 1572872 | tf_op jit(solution)/shard_map/ppermute | solution.py:39
  239.9 18.1 %collective-permute-start.21 = (bf16[64,2048]{1,0:T(8,128)(2,1)S(1)}, bf16[64,2048]{1,0:T(8,128)(2,1)S(1)}, u32[]{:S(2)}, u32[]{:S(2)}) collective-permute-start(bf16[64,2048]{1,0:T(8,128)(2,1)S(1)} %get-tuple-element.266), channel_id=1, source_target_pairs={{0,1},{1,2},{2,3},{3,0},{4,5},{5,6},{6,7},{7,4},{8,9},{9,10},{10,1... | collective-permute-start | bytes 786440 | tf_op jit(solution)/shard_map/ppermute | solution.py:47
  241.4 16.7 %collective-permute-start.22 = (bf16[64,2048]{1,0:T(8,128)(2,1)S(1)}, bf16[64,2048]{1,0:T(8,128)(2,1)S(1)}, u32[]{:S(2)}, u32[]{:S(2)}) collective-permute-start(bf16[64,2048]{1,0:T(8,128)(2,1)S(1)} %get-tuple-element.267), channel_id=1, source_target_pairs={{0,3},{1,0},{2,1},{3,2},{4,7},{5,4},{6,5},{7,6},{8,11},{9,8},{10,9... | collective-permute-start | bytes 786440 | tf_op jit(solution)/shard_map/ppermute | solution.py:47
  243.2 14.9 %collective-permute-start.23 = (bf16[64,2048]{1,0:T(8,128)(2,1)S(1)}, bf16[64,2048]{1,0:T(8,128)(2,1)S(1)}, u32[]{:S(2)}, u32[]{:S(2)}) collective-permute-start(bf16[64,2048]{1,0:T(8,128)(2,1)S(1)} %get-tuple-element.268), channel_id=1, source_target_pairs={{0,2},{1,3},{2,0},{3,1},{4,6},{5,7},{6,4},{7,5},{8,10},{9,11},{10,... | collective-permute-start | bytes 786440 | tf_op jit(solution)/shard_map/ppermute | solution.py:47
  263.1 12.8 %collective-permute-start.25 = (bf16[1024,512]{1,0:T(8,128)(2,1)S(1)}, bf16[1024,512]{1,0:T(8,128)(2,1)S(1)}, u32[]{:S(2)}, u32[]{:S(2)}) collective-permute-start(bf16[1024,512]{1,0:T(8,128)(2,1)S(1)} %get-tuple-element.278), channel_id=1, source_target_pairs={{0,8},{8,0},{16,24},{24,16},{1,9},{9,1},{17,25},{25,17},{2,10},{10... | collective-permute-start | bytes 3145736 | tf_op jit(solution)/shard_map/ppermute | solution.py:23
  263.3 12.0 %collective-permute-start.26 = (bf16[64,2048]{1,0:T(8,128)(2,1)S(1)}, bf16[64,2048]{1,0:T(8,128)(2,1)S(1)}, u32[]{:S(2)}, u32[]{:S(2)}) collective-permute-start(bf16[64,2048]{1,0:T(8,128)(2,1)S(1)} %shard_map.219.refs_0_), channel_id=1, source_target_pairs={{0,4},{1,5},{2,6},{3,7},{4,0},{5,1},{6,2},{7,3},{8,12},{9,13},{10,... | collective-permute-start | bytes 786440 | tf_op jit(solution)/shard_map/ppermute | solution.py:39
  282.6 14.1 %collective-permute-start.30 = (bf16[512,512]{1,0:T(8,128)(2,1)S(1)}, bf16[512,512]{1,0:T(8,128)(2,1)S(1)}, u32[]{:S(2)}, u32[]{:S(2)}) collective-permute-start(bf16[512,512]{1,0:T(8,128)(2,1)S(1)} %shard_map.222), channel_id=1, source_target_pairs={{0,16},{8,24},{16,0},{24,8},{1,17},{9,25},{17,1},{25,9},{2,18},{10... | collective-permute-start | bytes 1572872 | tf_op jit(solution)/shard_map/ppermute | solution.py:27
  296.7 65.6 %reduce-scatter.9.cloned.1.call-start = ((), (), s32[]{:S(2)}) async-start(), calls=%async_computation.10 | async-start | bytes 2621440 | tf_op jit(solution)/shard_map/reduce_scatter | solution.py:896
  297.3 142.3 %reduce-scatter.11.cloned.1.call-start = ((), (), s32[]{:S(2)}) async-start(), calls=%async_computation.11 | async-start | bytes 1966080 | tf_op jit(solution)/shard_map/reduce_scatter | solution.py:896
  311.5 19.1 %collective-permute-start.36 = (bf16[128,2048]{1,0:T(8,128)(2,1)S(1)}, bf16[128,2048]{1,0:T(8,128)(2,1)S(1)}, u32[]{:S(2)}, u32[]{:S(2)}) collective-permute-start(bf16[128,2048]{1,0:T(8,128)(2,1)S(1)} %get-tuple-element.307), channel_id=1, source_target_pairs={{0,4},{1,5},{2,6},{3,7},{4,0},{5,1},{6,2},{7,3},{8,12},{9,13},{10,... | collective-permute-start | bytes 1572872 | tf_op jit(solution)/shard_map/ppermute | solution.py:39
  314.6 13.4 %collective-permute-start.34 = (bf16[64,2048]{1,0:T(8,128)(2,1)S(1)}, bf16[64,2048]{1,0:T(8,128)(2,1)S(1)}, u32[]{:S(2)}, u32[]{:S(2)}) collective-permute-start(bf16[64,2048]{1,0:T(8,128)(2,1)S(1)} %get-tuple-element.305), channel_id=1, source_target_pairs={{0,3},{1,0},{2,1},{3,2},{4,7},{5,4},{6,5},{7,6},{8,11},{9,8},{10,9... | collective-permute-start | bytes 786440 | tf_op jit(solution)/shard_map/ppermute | solution.py:47
  317.3 12.5 %collective-permute-start.35 = (bf16[64,2048]{1,0:T(8,128)(2,1)S(1)}, bf16[64,2048]{1,0:T(8,128)(2,1)S(1)}, u32[]{:S(2)}, u32[]{:S(2)}) collective-permute-start(bf16[64,2048]{1,0:T(8,128)(2,1)S(1)} %get-tuple-element.306), channel_id=1, source_target_pairs={{0,2},{1,3},{2,0},{3,1},{4,6},{5,7},{6,4},{7,5},{8,10},{9,11},{10,... | collective-permute-start | bytes 786440 | tf_op jit(solution)/shard_map/ppermute | solution.py:47
  331.3 19.6 %collective-permute-start.41 = (bf16[1024,768]{1,0:T(8,128)(2,1)S(1)}, bf16[1024,768]{1,0:T(8,128)(2,1)S(1)}, u32[]{:S(2)}, u32[]{:S(2)}) collective-permute-start(bf16[1024,768]{1,0:T(8,128)(2,1)S(1)} %shard_map.227), channel_id=1, source_target_pairs={{0,8},{8,0},{16,24},{24,16},{1,9},{9,1},{17,25},{25,17},{2,10},{10... | collective-permute-start | bytes 4718600 | tf_op jit(solution)/shard_map/ppermute | solution.py:23
  333.6 10.9 %collective-permute-start.38 = (bf16[32,2048]{1,0:T(8,128)(2,1)S(1)}, bf16[32,2048]{1,0:T(8,128)(2,1)S(1)}, u32[]{:S(2)}, u32[]{:S(2)}) collective-permute-start(bf16[32,2048]{1,0:T(8,128)(2,1)S(1)} %get-tuple-element.317), channel_id=1, source_target_pairs={{0,1},{1,2},{2,3},{3,0},{4,5},{5,6},{6,7},{7,4},{8,9},{9,10},{10,1... | collective-permute-start | bytes 393224 | tf_op jit(solution)/shard_map/ppermute | solution.py:47
  338.7 12.3 %collective-permute-start.37 = (bf16[64,2048]{1,0:T(8,128)(2,1)S(1)}, bf16[64,2048]{1,0:T(8,128)(2,1)S(1)}, u32[]{:S(2)}, u32[]{:S(2)}) collective-permute-start(bf16[64,2048]{1,0:T(8,128)(2,1)S(1)} %shard_map.229.refs_0_), channel_id=1, source_target_pairs={{0,4},{1,5},{2,6},{3,7},{4,0},{5,1},{6,2},{7,3},{8,12},{9,13},{10,... | collective-permute-start | bytes 786440 | tf_op jit(solution)/shard_map/ppermute | solution.py:39
  342.2 20.1 %collective-permute-start.45 = (bf16[128,1280]{1,0:T(8,128)(2,1)}, bf16[128,1280]{1,0:T(8,128)(2,1)}, u32[]{:S(2)}, u32[]{:S(2)}) collective-permute-start(bf16[128,1280]{1,0:T(8,128)(2,1)} %slice.52), channel_id=1, source_target_pairs={{0,16},{8,24},{16,0},{24,8},{1,17},{9,25},{17,1},{25,9},{2,18},{10... | collective-permute-start | bytes 983048 | tf_op jit(solution)/shard_map/ppermute | solution.py:27
  351.1 11.2 %collective-permute-start.42 = (bf16[32,2048]{1,0:T(8,128)(2,1)S(1)}, bf16[32,2048]{1,0:T(8,128)(2,1)S(1)}, u32[]{:S(2)}, u32[]{:S(2)}) collective-permute-start(bf16[32,2048]{1,0:T(8,128)(2,1)S(1)} %shard_map.230.refs_0_), channel_id=1, source_target_pairs={{1,0},{2,1},{3,2},{0,3},{5,4},{6,5},{7,6},{4,7},{9,8},{10,9},{11,1... | collective-permute-start | bytes 393224 | tf_op jit(solution)/shard_map/ppermute | solution.py:43
  362.4 20.7 %collective-permute-start.50 = (bf16[128,2048]{1,0:T(8,128)(2,1)S(1)}, bf16[128,2048]{1,0:T(8,128)(2,1)S(1)}, u32[]{:S(2)}, u32[]{:S(2)}) collective-permute-start(bf16[128,2048]{1,0:T(8,128)(2,1)S(1)} %shard_map.233.rest_4_), channel_id=1, source_target_pairs={{0,4},{1,5},{2,6},{3,7},{4,0},{5,1},{6,2},{7,3},{8,12},{9,13},{10,... | collective-permute-start | bytes 1572872 | tf_op jit(solution)/shard_map/ppermute | solution.py:39
  365.5 13.9 %collective-permute-start.47 = (bf16[64,2048]{1,0:T(8,128)(2,1)S(1)}, bf16[64,2048]{1,0:T(8,128)(2,1)S(1)}, u32[]{:S(2)}, u32[]{:S(2)}) collective-permute-start(bf16[64,2048]{1,0:T(8,128)(2,1)S(1)} %shard_map.231.rest_0_), channel_id=1, source_target_pairs={{1,0},{2,1},{3,2},{0,3},{5,4},{6,5},{7,6},{4,7},{9,8},{10,9},{11,1... | collective-permute-start | bytes 786440 | tf_op jit(solution)/shard_map/ppermute | solution.py:43
  368.4 11.0 %collective-permute-start.48 = (bf16[64,2048]{1,0:T(8,128)(2,1)S(1)}, bf16[64,2048]{1,0:T(8,128)(2,1)S(1)}, u32[]{:S(2)}, u32[]{:S(2)}) collective-permute-start(bf16[64,2048]{1,0:T(8,128)(2,1)S(1)} %shard_map.231.rest_0_), channel_id=1, source_target_pairs={{2,0},{3,1},{0,2},{1,3},{6,4},{7,5},{4,6},{5,7},{10,8},{11,9},{8,1... | collective-permute-start | bytes 786440 | tf_op jit(solution)/shard_map/ppermute | solution.py:43
  369.1 14.0 %collective-permute-start.49 = (bf16[64,2048]{1,0:T(8,128)(2,1)S(1)}, bf16[64,2048]{1,0:T(8,128)(2,1)S(1)}, u32[]{:S(2)}, u32[]{:S(2)}) collective-permute-start(bf16[64,2048]{1,0:T(8,128)(2,1)S(1)} %shard_map.231.rest_0_), channel_id=1, source_target_pairs={{3,0},{0,1},{1,2},{2,3},{7,4},{4,5},{5,6},{6,7},{11,8},{8,9},{9,10... | collective-permute-start | bytes 786440 | tf_op jit(solution)/shard_map/ppermute | solution.py:43
  371.0 28.0 %collective-permute-start.46 = (bf16[128,1024]{1,0:T(8,128)(2,1)S(1)}, bf16[128,1024]{1,0:T(8,128)(2,1)S(1)}, u32[]{:S(2)}, u32[]{:S(2)}) collective-permute-start(bf16[128,1024]{1,0:T(8,128)(2,1)S(1)} %slice.53), channel_id=1, source_target_pairs={{0,16},{8,24},{16,0},{24,8},{1,17},{9,25},{17,1},{25,9},{2,18},{10... | collective-permute-start | bytes 786440 | tf_op jit(solution)/shard_map/ppermute | solution.py:27
  404.8 11.7 %collective-permute-start.51 = (bf16[1024,512]{1,0:T(8,128)(2,1)S(1)}, bf16[1024,512]{1,0:T(8,128)(2,1)S(1)}, u32[]{:S(2)}, u32[]{:S(2)}) collective-permute-start(bf16[1024,512]{1,0:T(8,128)(2,1)S(1)} %get-tuple-element.340), channel_id=1, source_target_pairs={{0,8},{8,0},{16,24},{24,16},{1,9},{9,1},{17,25},{25,17},{2,10},{10... | collective-permute-start | bytes 3145736 | tf_op jit(solution)/shard_map/ppermute | solution.py:23
  416.5 62.4 %reduce-scatter.13.cloned.1.call-start = ((), (), s32[]{:S(2)}) async-start(), calls=%async_computation.12 | async-start | bytes 3276800 | tf_op jit(solution)/shard_map/reduce_scatter | solution.py:896
  423.1 14.4 %collective-permute-start.55 = (bf16[512,512]{1,0:T(8,128)(2,1)S(1)}, bf16[512,512]{1,0:T(8,128)(2,1)S(1)}, u32[]{:S(2)}, u32[]{:S(2)}) collective-permute-start(bf16[512,512]{1,0:T(8,128)(2,1)S(1)} %shard_map.238), channel_id=1, source_target_pairs={{0,16},{8,24},{16,0},{24,8},{1,17},{9,25},{17,1},{25,9},{2,18},{10... | collective-permute-start | bytes 1572872 | tf_op jit(solution)/shard_map/ppermute | solution.py:27
  439.6 80.6 %reduce-scatter.15.cloned.1.call-start = ((), (), s32[]{:S(2)}) async-start(), calls=%async_computation.13 | async-start | bytes 2621440 | tf_op jit(solution)/shard_map/reduce_scatter | solution.py:896
  440.3 99.8 %reduce-scatter.17.cloned.1.call-start = ((), (), s32[]{:S(2)}) async-start(), calls=%async_computation.14 | async-start | bytes 1966080 | tf_op jit(solution)/shard_map/reduce_scatter | solution.py:896
  440.5 22.3 %collective-permute-start.62 = (bf16[64,2048]{1,0:T(8,128)(2,1)S(1)}, bf16[64,2048]{1,0:T(8,128)(2,1)S(1)}, u32[]{:S(2)}, u32[]{:S(2)}) collective-permute-start(bf16[64,2048]{1,0:T(8,128)(2,1)S(1)} %shard_map.243.rest_1_), channel_id=1, source_target_pairs={{1,0},{2,1},{3,2},{0,3},{5,4},{6,5},{7,6},{4,7},{9,8},{10,9},{11,1... | collective-permute-start | bytes 786440 | tf_op jit(solution)/shard_map/ppermute | solution.py:43
  443.5 21.2 %collective-permute-start.63 = (bf16[64,2048]{1,0:T(8,128)(2,1)S(1)}, bf16[64,2048]{1,0:T(8,128)(2,1)S(1)}, u32[]{:S(2)}, u32[]{:S(2)}) collective-permute-start(bf16[64,2048]{1,0:T(8,128)(2,1)S(1)} %shard_map.243.rest_1_), channel_id=1, source_target_pairs={{3,0},{0,1},{1,2},{2,3},{7,4},{4,5},{5,6},{6,7},{11,8},{8,9},{9,10... | collective-permute-start | bytes 786440 | tf_op jit(solution)/shard_map/ppermute | solution.py:43
  443.7 23.1 %collective-permute-start.64 = (bf16[64,2048]{1,0:T(8,128)(2,1)S(1)}, bf16[64,2048]{1,0:T(8,128)(2,1)S(1)}, u32[]{:S(2)}, u32[]{:S(2)}) collective-permute-start(bf16[64,2048]{1,0:T(8,128)(2,1)S(1)} %shard_map.243.rest_1_), channel_id=1, source_target_pairs={{2,0},{3,1},{0,2},{1,3},{6,4},{7,5},{4,6},{5,7},{10,8},{11,9},{8,1... | collective-permute-start | bytes 786440 | tf_op jit(solution)/shard_map/ppermute | solution.py:43
  445.9 22.2 %collective-permute-start.65 = (bf16[128,2048]{1,0:T(8,128)(2,1)S(1)}, bf16[128,2048]{1,0:T(8,128)(2,1)S(1)}, u32[]{:S(2)}, u32[]{:S(2)}) collective-permute-start(bf16[128,2048]{1,0:T(8,128)(2,1)S(1)} %shard_map.244.rest_5_), channel_id=1, source_target_pairs={{0,4},{1,5},{2,6},{3,7},{4,0},{5,1},{6,2},{7,3},{8,12},{9,13},{10,... | collective-permute-start | bytes 1572872 | tf_op jit(solution)/shard_map/ppermute | solution.py:39
  462.4 15.7 %collective-permute-start.61 = (bf16[128,2048]{1,0:T(8,128)(2,1)S(1)}, bf16[128,2048]{1,0:T(8,128)(2,1)S(1)}, u32[]{:S(2)}, u32[]{:S(2)}) collective-permute-start(bf16[128,2048]{1,0:T(8,128)(2,1)S(1)} %get-tuple-element.363), channel_id=1, source_target_pairs={{0,4},{1,5},{2,6},{3,7},{4,0},{5,1},{6,2},{7,3},{8,12},{9,13},{10,... | collective-permute-start | bytes 1572872 | tf_op jit(solution)/shard_map/ppermute | solution.py:39
  462.8 13.2 %collective-permute-start.58 = (bf16[64,2048]{1,0:T(8,128)(2,1)S(1)}, bf16[64,2048]{1,0:T(8,128)(2,1)S(1)}, u32[]{:S(2)}, u32[]{:S(2)}) collective-permute-start(bf16[64,2048]{1,0:T(8,128)(2,1)S(1)} %get-tuple-element.360), channel_id=1, source_target_pairs={{0,1},{1,2},{2,3},{3,0},{4,5},{5,6},{6,7},{7,4},{8,9},{9,10},{10,1... | collective-permute-start | bytes 786440 | tf_op jit(solution)/shard_map/ppermute | solution.py:47
  465.4 11.4 %collective-permute-start.59 = (bf16[64,2048]{1,0:T(8,128)(2,1)S(1)}, bf16[64,2048]{1,0:T(8,128)(2,1)S(1)}, u32[]{:S(2)}, u32[]{:S(2)}) collective-permute-start(bf16[64,2048]{1,0:T(8,128)(2,1)S(1)} %get-tuple-element.361), channel_id=1, source_target_pairs={{0,3},{1,0},{2,1},{3,2},{4,7},{5,4},{6,5},{7,6},{8,11},{9,8},{10,9... | collective-permute-start | bytes 786440 | tf_op jit(solution)/shard_map/ppermute | solution.py:47
  467.5 10.0 %collective-permute-start.60 = (bf16[64,2048]{1,0:T(8,128)(2,1)S(1)}, bf16[64,2048]{1,0:T(8,128)(2,1)S(1)}, u32[]{:S(2)}, u32[]{:S(2)}) collective-permute-start(bf16[64,2048]{1,0:T(8,128)(2,1)S(1)} %get-tuple-element.362), channel_id=1, source_target_pairs={{0,2},{1,3},{2,0},{3,1},{4,6},{5,7},{6,4},{7,5},{8,10},{9,11},{10,... | collective-permute-start | bytes 786440 | tf_op jit(solution)/shard_map/ppermute | solution.py:47
  479.0 21.4 %collective-permute-start.70 = (bf16[1024,768]{1,0:T(8,128)(2,1)S(1)}, bf16[1024,768]{1,0:T(8,128)(2,1)S(1)}, u32[]{:S(2)}, u32[]{:S(2)}) collective-permute-start(bf16[1024,768]{1,0:T(8,128)(2,1)S(1)} %shard_map.245), channel_id=1, source_target_pairs={{0,8},{8,0},{16,24},{24,16},{1,9},{9,1},{17,25},{25,17},{2,10},{10... | collective-permute-start | bytes 4718600 | tf_op jit(solution)/shard_map/ppermute | solution.py:23
  479.0 11.6 %collective-permute-start.71 = (f32[2,8,2048]{2,1,0:T(8,128)S(1)}, f32[2,8,2048]{2,1,0:T(8,128)S(1)}, u32[]{:S(2)}, u32[]{:S(2)}) collective-permute-start(f32[2,8,2048]{2,1,0:T(8,128)S(1)} %pad_maximum_fusion.1), channel_id=1, source_target_pairs={{0,16},{8,24},{16,0},{24,8},{1,17},{9,25},{17,1},{25,9},{2,18},{10... | collective-permute-start | bytes 393224 | tf_op jit(solution)/shard_map/ppermute | solution.py:27
  480.6 10.1 %collective-permute-start.72 = (f32[2,8,2048]{2,1,0:T(8,128)S(1)}, f32[2,8,2048]{2,1,0:T(8,128)S(1)}, u32[]{:S(2)}, u32[]{:S(2)}) collective-permute-start(f32[2,8,2048]{2,1,0:T(8,128)S(1)} %pad_maximum_fusion.1), channel_id=1, source_target_pairs={{0,8},{8,0},{16,24},{24,16},{1,9},{9,1},{17,25},{25,17},{2,10},{10... | collective-permute-start | bytes 393224 | tf_op jit(solution)/shard_map/ppermute | solution.py:23
  480.8 13.1 %collective-permute-start.73 = (f32[2,8,2048]{2,1,0:T(8,128)S(1)}, f32[2,8,2048]{2,1,0:T(8,128)S(1)}, u32[]{:S(2)}, u32[]{:S(2)}) collective-permute-start(f32[2,8,2048]{2,1,0:T(8,128)S(1)} %pad_maximum_fusion.1), channel_id=1, source_target_pairs={{0,24},{8,16},{16,8},{24,0},{1,25},{9,17},{17,9},{25,1},{2,26},{10... | collective-permute-start | bytes 393224 | tf_op jit(solution)/shard_map/ppermute | solution.py:35
  485.1 15.3 %collective-permute-start.66 = (bf16[64,2048]{1,0:T(8,128)(2,1)S(1)}, bf16[64,2048]{1,0:T(8,128)(2,1)S(1)}, u32[]{:S(2)}, u32[]{:S(2)}) collective-permute-start(bf16[64,2048]{1,0:T(8,128)(2,1)S(1)} %shard_map.247.refs_0_), channel_id=1, source_target_pairs={{0,4},{1,5},{2,6},{3,7},{4,0},{5,1},{6,2},{7,3},{8,12},{9,13},{10,... | collective-permute-start | bytes 786440 | tf_op jit(solution)/shard_map/ppermute | solution.py:39
  506.1 11.1 %collective-permute-start.81 = (bf16[128,1280]{1,0:T(8,128)(2,1)S(1)}, bf16[128,1280]{1,0:T(8,128)(2,1)S(1)}, u32[]{:S(2)}, u32[]{:S(2)}) collective-permute-start(bf16[128,1280]{1,0:T(8,128)(2,1)S(1)} %slice.55), channel_id=1, source_target_pairs={{0,16},{8,24},{16,0},{24,8},{1,17},{9,25},{17,1},{25,9},{2,18},{10... | collective-permute-start | bytes 983048 | tf_op jit(solution)/shard_map/ppermute | solution.py:27
  507.3 11.4 %collective-permute-start.74 = (bf16[32,2048]{1,0:T(8,128)(2,1)S(1)}, bf16[32,2048]{1,0:T(8,128)(2,1)S(1)}, u32[]{:S(2)}, u32[]{:S(2)}) collective-permute-start(bf16[32,2048]{1,0:T(8,128)(2,1)S(1)} %shard_map.248.refs_0_), channel_id=1, source_target_pairs={{1,0},{2,1},{3,2},{0,3},{5,4},{6,5},{7,6},{4,7},{9,8},{10,9},{11,1... | collective-permute-start | bytes 393224 | tf_op jit(solution)/shard_map/ppermute | solution.py:43
  510.0 11.2 %collective-permute-start.75 = (bf16[32,2048]{1,0:T(8,128)(2,1)S(1)}, bf16[32,2048]{1,0:T(8,128)(2,1)S(1)}, u32[]{:S(2)}, u32[]{:S(2)}) collective-permute-start(bf16[32,2048]{1,0:T(8,128)(2,1)S(1)} %shard_map.248.refs_0_), channel_id=1, source_target_pairs={{3,0},{0,1},{1,2},{2,3},{7,4},{4,5},{5,6},{6,7},{11,8},{8,9},{9,10... | collective-permute-start | bytes 393224 | tf_op jit(solution)/shard_map/ppermute | solution.py:43
  510.0 11.9 %collective-permute-start.76 = (bf16[32,2048]{1,0:T(8,128)(2,1)S(1)}, bf16[32,2048]{1,0:T(8,128)(2,1)S(1)}, u32[]{:S(2)}, u32[]{:S(2)}) collective-permute-start(bf16[32,2048]{1,0:T(8,128)(2,1)S(1)} %shard_map.248.refs_0_), channel_id=1, source_target_pairs={{2,0},{3,1},{0,2},{1,3},{6,4},{7,5},{4,6},{5,7},{10,8},{11,9},{8,1... | collective-permute-start | bytes 393224 | tf_op jit(solution)/shard_map/ppermute | solution.py:43
  521.2 11.8 %collective-permute-start.89 = (bf16[128,1024]{1,0:T(8,128)(2,1)S(1)}, bf16[128,1024]{1,0:T(8,128)(2,1)S(1)}, u32[]{:S(2)}, u32[]{:S(2)}) collective-permute-start(bf16[128,1024]{1,0:T(8,128)(2,1)S(1)} %slice.69), channel_id=1, source_target_pairs={{0,16},{8,24},{16,0},{24,8},{1,17},{9,25},{17,1},{25,9},{2,18},{10... | collective-permute-start | bytes 786440 | tf_op jit(solution)/shard_map/ppermute | solution.py:27
  528.0 24.4 %collective-permute-start.82 = (bf16[128,2048]{1,0:T(8,128)(2,1)S(1)}, bf16[128,2048]{1,0:T(8,128)(2,1)S(1)}, u32[]{:S(2)}, u32[]{:S(2)}) collective-permute-start(bf16[128,2048]{1,0:T(8,128)(2,1)S(1)} %shard_map.251.rest_6_), channel_id=1, source_target_pairs={{0,4},{1,5},{2,6},{3,7},{4,0},{5,1},{6,2},{7,3},{8,12},{9,13},{10,... | collective-permute-start | bytes 1572872 | tf_op jit(solution)/shard_map/ppermute | solution.py:39
  532.3 20.0 %collective-permute-start.83 = (bf16[64,2048]{1,0:T(8,128)(2,1)S(1)}, bf16[64,2048]{1,0:T(8,128)(2,1)S(1)}, u32[]{:S(2)}, u32[]{:S(2)}) collective-permute-start(bf16[64,2048]{1,0:T(8,128)(2,1)S(1)} %shard_map.249.rest_2_), channel_id=1, source_target_pairs={{1,0},{2,1},{3,2},{0,3},{5,4},{6,5},{7,6},{4,7},{9,8},{10,9},{11,1... | collective-permute-start | bytes 786440 | tf_op jit(solution)/shard_map/ppermute | solution.py:43
  532.9 19.4 %collective-permute-start.84 = (bf16[64,2048]{1,0:T(8,128)(2,1)S(1)}, bf16[64,2048]{1,0:T(8,128)(2,1)S(1)}, u32[]{:S(2)}, u32[]{:S(2)}) collective-permute-start(bf16[64,2048]{1,0:T(8,128)(2,1)S(1)} %shard_map.249.rest_2_), channel_id=1, source_target_pairs={{3,0},{0,1},{1,2},{2,3},{7,4},{4,5},{5,6},{6,7},{11,8},{8,9},{9,10... | collective-permute-start | bytes 786440 | tf_op jit(solution)/shard_map/ppermute | solution.py:43
  535.5 16.9 %collective-permute-start.85 = (bf16[64,2048]{1,0:T(8,128)(2,1)S(1)}, bf16[64,2048]{1,0:T(8,128)(2,1)S(1)}, u32[]{:S(2)}, u32[]{:S(2)}) collective-permute-start(bf16[64,2048]{1,0:T(8,128)(2,1)S(1)} %shard_map.249.rest_2_), channel_id=1, source_target_pairs={{2,0},{3,1},{0,2},{1,3},{6,4},{7,5},{4,6},{5,7},{10,8},{11,9},{8,1... | collective-permute-start | bytes 786440 | tf_op jit(solution)/shard_map/ppermute | solution.py:43
  552.7 15.0 %collective-permute-start.91 = (f32[2,4,2048]{2,1,0:T(4,128)S(1)}, f32[2,4,2048]{2,1,0:T(4,128)S(1)}, u32[]{:S(2)}, u32[]{:S(2)}) collective-permute-start(f32[2,4,2048]{2,1,0:T(4,128)S(1)} %add_add_fusion.2), channel_id=1, source_target_pairs={{0,4},{1,5},{2,6},{3,7},{4,0},{5,1},{6,2},{7,3},{8,12},{9,13},{10,... | collective-permute-start | bytes 196616 | tf_op jit(solution)/shard_map/ppermute | solution.py:39
  (176 other events, 1632.9 us)
Sparse Core Ops, SparseCore 0:
  10.2 74.2 all-gather.3
  110.8 64.8 all-gather.5
  177.9 46.5 all-gather.7
  296.8 33.7 reduce-scatter.6
  332.9 29.3 reduce-scatter.8
  416.7 22.8 reduce-scatter.10
  442.7 33.6 reduce-scatter.12
  479.5 29.3 reduce-scatter.14
  511.9 26.8 reduce-scatter.16
